TPU v7x, 128 devices: a whole 4x4x4 slice. The times are simulated.
128 devices in a mesh: dom: 64 (over x, z, y), rep: 2 (over core).
Axes of the slice: x: 4, y: 4, z: 4, core: 2. Of those that a mesh axis runs over, the one named last changes fastest.
Arguments:
- features: bfloat16 [524288, 128], P('dom', 'rep'), may hold values from -6 to 6
- weight_first: bfloat16 [128, 256], P(None, 'rep'), may hold values from -0.5 to 0.5
- weight_second: bfloat16 [256, 47], P('rep'), may hold values from -1.5 to 1.5
- labels: int32 [524288], P('dom'), may hold values from 0 to 46
- send_index: int32 [64, 64, 2], P('dom'), may hold values from -1 to 63, as said below
- tile_src: int32 [16384], P('dom'), may hold values from 0 to 191, as said below
- tile_dst: int32 [16384], P('dom'), may hold values from 0 to 63, as said below
- tile_values: bfloat16 [16384, 128, 128], P('dom'), may hold values from -0.25 to 0.25
Outputs:
- hidden: bfloat16 [524288, 256], P('dom', 'rep')
- grad_first: float32 [128, 256], P(None, 'rep')
- grad_second: float32 [256, 47], P('rep')
- loss: float32 [], replicated
Inputs may be any that keep to these rules, and one draw needn't show every extreme that they name: `send_index`: entry [s, r, j] names a local row block of partition s read by partition r in slot j; -1 marks an empty slot; the used slots of a pair come first; no partition reads from itself; a partition reads at most 2 blocks from each other one, many pairs use fewer or none; one hub partition reads 2 blocks from every other one. `tile_src`: the first 64 tiles of each partition map its block b onto its block b; every other tile names an own block or a used slot; each used slot is named by at least one tile. `tile_dst`: the first 64 tiles of each partition have destinations 0 to 63 in order.
All inputs are finite; a program needn't handle non-finite values.
Results may differ from a plain program's by a relative error of at most 0.006.
Values may be sent and summed in bfloat16 or wider, within the bound.
A program may use at most 192 MiB of HBM per device.

v0:
```python
import jax
import jax.numpy as jnp
from jax import lax
from jax.sharding import PartitionSpec as P

BLK = 128
NB = 64
S = 2


def outgoing(node_rows, send_index):
    width_cols = node_rows.shape[-1]
    blocks = node_rows.reshape(NB, BLK, width_cols)
    slot_index = send_index[0]
    chosen = blocks[jnp.clip(slot_index, 0, NB - 1)]
    return jnp.where((slot_index >= 0)[:, :, None, None], chosen, jnp.zeros((), node_rows.dtype))


def build_table(node_rows, received):
    width_cols = node_rows.shape[-1]
    return jnp.concatenate(
        [node_rows.reshape(NB, BLK, width_cols), received.reshape(-1, BLK, width_cols)], axis=0
    )


def aggregate(block_table, tile_src, tile_dst, tile_values):
    gathered = block_table[tile_src]
    products = jnp.einsum("tij,tjw->tiw", tile_values, gathered, preferred_element_type=jnp.float32)
    summed = jax.ops.segment_sum(products, tile_dst, num_segments=NB)
    return summed.reshape(NB * BLK, -1)


def split_product(mixed_rows, masked_rows):
    upper_part = masked_rows.astype(jnp.bfloat16)
    lower_part = (masked_rows - upper_part.astype(jnp.float32)).astype(jnp.bfloat16)
    first_term = jnp.einsum("rf,rh->fh", mixed_rows, upper_part, preferred_element_type=jnp.float32)
    second_term = jnp.einsum(
        "rf,rh->fh", mixed_rows, lower_part, preferred_element_type=jnp.float32
    )
    return first_term + second_term


def per_device(
    features, weight_first, weight_second, labels, send_index, tile_src, tile_dst, tile_values
):
    dom_count = lax.axis_size("dom")
    node_count = dom_count * NB * BLK
    half_hidden = weight_first.shape[1]
    got_features = lax.all_to_all(
        outgoing(features, send_index), "dom", split_axis=0, concat_axis=0, tiled=True
    )
    first_mixed = aggregate(
        build_table(features, got_features), tile_src, tile_dst, tile_values
    ).astype(jnp.bfloat16)
    mixed_full = lax.all_gather(first_mixed, "rep", axis=1, tiled=True)
    pre_act = jnp.dot(mixed_full, weight_first, preferred_element_type=jnp.float32)
    hidden = jnp.maximum(pre_act, 0.0).astype(jnp.bfloat16)
    got_hidden = lax.all_to_all(
        outgoing(hidden, send_index), "dom", split_axis=0, concat_axis=0, tiled=True
    )
    hidden_table = build_table(hidden, got_hidden)
    second_mixed = aggregate(hidden_table, tile_src, tile_dst, tile_values).astype(jnp.bfloat16)
    logits = lax.psum(
        jnp.dot(second_mixed, weight_second, preferred_element_type=jnp.float32).astype(
            jnp.bfloat16
        ),
        "rep",
    ).astype(jnp.float32)
    log_total = jnp.log(jnp.sum(jnp.exp(logits), axis=-1))
    onehot = (labels[:, None] == jnp.arange(logits.shape[1], dtype=jnp.int32)[None, :]).astype(
        jnp.float32
    )
    loss_local = jnp.sum(log_total - jnp.sum(logits * onehot, axis=-1))
    softmax_probs = jnp.exp(logits - log_total[:, None])
    grad_logits = ((softmax_probs - onehot) * (1.0 / node_count**0.5)).astype(jnp.bfloat16)
    grad_second = jnp.einsum(
        "rh,rc->hc", second_mixed, grad_logits, preferred_element_type=jnp.float32
    )
    grad_mixed = jnp.einsum(
        "rc,hc->rh", grad_logits, weight_second, preferred_element_type=jnp.float32
    ).astype(jnp.bfloat16)
    grad_blocks = grad_mixed.reshape(NB, BLK, half_hidden)
    products = jnp.einsum(
        "tij,tiw->tjw", tile_values, grad_blocks[tile_dst], preferred_element_type=jnp.float32
    )
    partial_value = jax.ops.segment_sum(products, tile_src, num_segments=NB + dom_count * S)
    returned = lax.all_to_all(
        partial_value[NB:].reshape(dom_count, S, BLK, half_hidden).astype(jnp.bfloat16),
        "dom",
        split_axis=0,
        concat_axis=0,
        tiled=True,
    ).astype(jnp.float32)
    slot_index = send_index[0].reshape(-1)
    target_block = jnp.where(slot_index >= 0, slot_index, NB)
    incoming = jax.ops.segment_sum(
        returned.reshape(-1, BLK, half_hidden), target_block, num_segments=NB + 1
    )[:NB]
    grad_hidden = (partial_value[:NB] + incoming).reshape(NB * BLK, half_hidden)
    masked = jnp.where(hidden > 0, grad_hidden, jnp.zeros((), jnp.float32))
    grad_first = split_product(mixed_full, masked)
    grad_first, grad_second, loss_total = lax.psum((grad_first, grad_second, loss_local), "dom")
    return (hidden, grad_first, grad_second, loss_total / node_count)


def solution(mesh):
    return jax.shard_map(
        per_device,
        mesh=mesh,
        in_specs=(
            P("dom", "rep"),
            P(None, "rep"),
            P("rep", None),
            P("dom"),
            P("dom", None, None),
            P("dom"),
            P("dom"),
            P("dom", None, None),
        ),
        out_specs=(P("dom", "rep"), P(None, "rep"), P("rep", None), P()),
        check_vma=False,
    )
```

profile of v0, /device:TPU:0, one launch (start us, length us, event | category | flops | bytes accessed | tf_op | source)
XLA Modules:
  0.0 895.0 jit_solution(14264871124864776837)
XLA Ops:
  7.2 0.0 copy-start
  7.2 0.8 compare_select_fusion.2
  8.0 0.7 compare_bitcast_fusion
  8.6 0.3 copy_bitcast_fusion.1
  8.9 0.1 copy.28
  9.0 0.1 reshape.104
  9.2 0.1 copy.27
  9.3 2.1 gather_fusion
  11.4 3.1 broadcast_select_fusion.1
  14.6 11.8 %all-to-all-start = ((bf16[64,2,128,64]{2,3,1,0:T(8,128)(2,1)}), bf16[64,2,128,64]{2,3,1,0:T(8,128)(2,1)}, u32[]{:S(2)}, u32[]{:S(2)}) async-start(bf16[64,2,128,64]{2,3,1,0:T(8,128)(2,1)} %broadcast_select_fusion.1), calls=%async_computation | async-start | bytes 4194304 | tf_op jit(solution)/shard_map/all_to_all | solution.py:49
  26.4 0.0 all-gather.2.cloned.1.call-start
  26.4 29.4 %all-to-all-done = bf16[64,2,128,64]{2,3,1,0:T(8,128)(2,1)} async-done(((bf16[64,2,128,64]{2,3,1,0:T(8,128)(2,1)}), bf16[64,2,128,64]{2,3,1,0:T(8,128)(2,1)}, u32[]{:S(2)}, u32[]{:S(2)}) %all-to-all-start) | async-done | bytes 2097184 | tf_op jit(solution)/shard_map/all_to_all | solution.py:49
  55.8 3.5 pad_maximum_fusion.1
  59.3 5.0 gather_fusion.1
  64.3 13.7 %convolution_bitcast_fusion.2 = f32[256,128,64]{1,2,0:T(8,128)} fusion(bf16[256,128,64]{1,2,0:T(8,128)(2,1)} %gather_fusion.1, bf16[256,128,128]{2,1,0:T(8,128)(2,1)} %param.15), kind=kOutput, calls=%fused_computation.22 | convolution fusion | flops 536870912 | bytes 20971520 | tf_op jit(solution)/shard_map/tij,tjw->tiw/dot_general | solution.py:28
  78.0 0.2 broadcast_in_dim.64
  78.3 26.1 %scatter_fusion = f32[64,128,64]{1,2,0:T(8,128)S(1)} fusion(f32[64,128,64]{1,2,0:T(8,128)S(1)} %broadcast_in_dim.64, s32[256]{0:T(256)S(1)} %copy-done.9, f32[256,128,64]{1,2,0:T(8,128)} %convolution_bitcast_fusion.2), kind=kCustom, calls=%fused_computation.5 | custom fusion | flops 2097152 | bytes 25166848 | tf_op jit(solution)/shard_map/scatter-add | solution.py:29
  104.4 1.1 copy_bitcast_fusion
  105.5 0.0 all-gather.2.cloned.1.call-update
  105.5 0.0 all-reduce.4.cloned.1.call-start
  105.6 9.6 %all-gather.2.cloned.1.call-done = bf16[8192,128]{0,1:T(8,128)(2,1)} async-done(((bf16[8192,64]{0,1:T(8,128)(2,1)}), bf16[8192,128]{0,1:T(8,128)(2,1)}) %all-gather.2.cloned.1.call-update) | async-done | bytes 2097168 | tf_op jit(solution)/shard_map/all_gather | solution.py:55
  115.2 2.3 fusion
  117.6 3.0 gather_fusion.2
  120.6 2.5 broadcast_select_fusion
  123.1 62.7 %all_to_all.15 = bf16[64,2,128,128]{3,2,1,0:T(8,128)(2,1)S(1)} all-to-all(bf16[64,2,128,128]{3,2,1,0:T(8,128)(2,1)S(1)} %broadcast_select_fusion), channel_id=1, replica_groups=mesh['dom'=64,'rep'=2] {'dom'}, dimensions={0} | all-to-all | bytes 8388608 | tf_op jit(solution)/shard_map/all_to_all | solution.py:58
  185.9 3.3 pad_maximum_fusion
  189.1 11.4 %gather_fusion.3 = bf16[256,128,128]{2,1,0:T(8,128)(2,1)} fusion(bf16[192,128,128]{2,1,0:T(8,128)(2,1)} %pad_maximum_fusion, s32[1024]{0:T(1024)S(1)} %pad_clamp_fusion.1), kind=kCustom, calls=%fused_computation.3 | custom fusion | bytes 16778240 | tf_op jit(solution)/shard_map/gather | solution.py:27
  200.5 12.8 %convolution_bitcast_fusion.1 = f32[256,128,128]{1,2,0:T(8,128)} fusion(bf16[256,128,128]{2,1,0:T(8,128)(2,1)} %gather_fusion.3, bf16[256,128,128]{2,1,0:T(8,128)(2,1)} %param.15), kind=kOutput, calls=%fused_computation.14 | convolution fusion | flops 1073741824 | bytes 33554432 | tf_op jit(solution)/shard_map/tij,tjw->tiw/dot_general | solution.py:28
  213.4 17.5 %copy.34 = f32[256,128,128]{2,1,0:T(8,128)} copy(f32[256,128,128]{1,2,0:T(8,128)} %convolution_bitcast_fusion.1) | data formatting | bytes 33554432 | tf_op jit(solution)/shard_map/tij,tjw->tiw/dot_general | solution.py:28
  230.8 2.4 broadcast_in_dim.71
  233.3 51.8 %scatter_fusion.1 = f32[64,128,128]{2,1,0:T(8,128)} fusion(f32[64,128,128]{2,1,0:T(8,128)} %broadcast_in_dim.71, s32[256]{0:T(256)S(1)} %copy-done.9, f32[256,128,128]{2,1,0:T(8,128)} %copy.34), kind=kCustom, calls=%fused_computation.6 | custom fusion | flops 4194304 | bytes 50332672 | tf_op jit(solution)/shard_map/scatter-add | solution.py:29
  285.1 2.6 convert_element_type.47
  287.7 1.4 copy-done.4
  289.0 1.7 convolution_convert_fusion.1
  290.8 0.0 all-reduce.4.cloned.1.call-update
  290.8 24.5 %all-reduce.4.cloned.1.call-done = bf16[8192,47]{0,1:T(8,128)(2,1)} async-done(((bf16[8192,47]{0,1:T(8,128)(2,1)}), bf16[8192,47]{0,1:T(8,128)(2,1)}) %all-reduce.4.cloned.1.call-update) | async-done | bytes 770064 | tf_op jit(solution)/shard_map/psum | solution.py:63
  315.3 1.6 fusion.7
  316.9 0.6 subtract_reduce_fusion
  317.5 3.3 convolution_convert_fusion
  320.8 10.2 %gather_fusion.4 = bf16[256,128,128]{2,1,0:T(8,128)(2,1)} fusion(bf16[64,128,128]{2,1,0:T(8,128)(2,1)} %bitcast.61, s32[1024]{0:T(1024)S(1)} %pad_clamp_fusion), kind=kCustom, calls=%fused_computation.4 | custom fusion | bytes 16778240 | tf_op jit(solution)/shard_map/gather | solution.py:84
  331.0 14.4 %convolution_bitcast_fusion = f32[256,128,128]{1,2,0:T(8,128)} fusion(bf16[256,128,128]{2,1,0:T(8,128)(2,1)} %gather_fusion.4, bf16[256,128,128]{2,1,0:T(8,128)(2,1)} %param.15), kind=kOutput, calls=%fused_computation.13 | convolution fusion | flops 1073741824 | bytes 33554432 | tf_op jit(solution)/shard_map/tij,tiw->tjw/dot_general | solution.py:83
  345.4 17.5 %copy.36 = f32[256,128,128]{2,1,0:T(8,128)} copy(f32[256,128,128]{1,2,0:T(8,128)} %convolution_bitcast_fusion) | data formatting | bytes 33554432 | tf_op jit(solution)/shard_map/tij,tiw->tjw/dot_general | solution.py:83
  362.9 6.2 broadcast_in_dim.69
  369.0 52.0 %scatter_fusion.2 = f32[192,128,128]{2,1,0:T(8,128)} fusion(f32[192,128,128]{2,1,0:T(8,128)} %broadcast_in_dim.69, s32[256]{0:T(256)S(1)} %copy-done.10, f32[256,128,128]{2,1,0:T(8,128)} %copy.36), kind=kCustom, calls=%fused_computation.7 | custom fusion | flops 4194304 | bytes 50332672 | tf_op jit(solution)/shard_map/scatter-add | solution.py:86
  421.0 6.3 slice.29
  427.3 10.9 %all-to-all-start.2 = ((bf16[64,2,128,128]{3,2,1,0:T(8,128)(2,1)}), bf16[64,2,128,128]{3,2,1,0:T(8,128)(2,1)}, u32[]{:S(2)}, u32[]{:S(2)}) async-start(bf16[64,2,128,128]{3,2,1,0:T(8,128)(2,1)} %bitcast.65), calls=%async_computation.2 | async-start | bytes 8388608 | tf_op jit(solution)/shard_map/all_to_all | solution.py:87
  438.3 0.0 all-reduce.6.cloned.1.call-start
  438.3 0.1 copy.37
  438.4 0.1 reshape_squeeze.3
  438.6 54.8 %all-to-all-done.2 = bf16[64,2,128,128]{3,2,1,0:T(8,128)(2,1)} async-done(((bf16[64,2,128,128]{3,2,1,0:T(8,128)(2,1)}), bf16[64,2,128,128]{3,2,1,0:T(8,128)(2,1)}, u32[]{:S(2)}, u32[]{:S(2)}) %all-to-all-start.2) | async-done | bytes 4194336 | tf_op jit(solution)/shard_map/all_to_all | solution.py:87
  493.4 6.5 bitcast_convert_fusion
  499.9 2.5 broadcast_in_dim.75
  502.4 26.6 %scatter_fusion.3 = f32[65,128,128]{2,1,0:T(8,128)} fusion(f32[65,128,128]{2,1,0:T(8,128)} %broadcast_in_dim.75, s32[128]{0:T(128)S(1)} %fusion.11, f32[128,128,128]{2,1,0:T(8,128)} %bitcast_convert_fusion), kind=kCustom, calls=%fused_computation.8 | custom fusion | flops 2097152 | bytes 25166336 | tf_op jit(solution)/shard_map/scatter-add | solution.py:96
  529.0 4.2 slice_add_fusion
  533.2 0.7 subtract_convert_fusion
  533.9 0.6 fusion.1
  534.6 1.0 copy-done.3
  535.5 0.7 fusion.14
  536.3 1.4 convolution_add_fusion
  537.7 0.0 all-reduce.6.cloned.1.call-update
  537.7 1.7 fusion.8
  539.4 345.7 %all-reduce = (f32[128,47]{0,1:T(8,128)}, f32[]{:T(128)}) all-reduce(f32[128,47]{0,1:T(8,128)S(1)} %fusion.8, f32[]{:T(128)} %get-tuple-element.8), channel_id=1, replica_groups=mesh['dom'=64,'rep'=2] {'dom'}, use_global_device_ids=true, to_apply=%region_7.8 | all-reduce | flops 6017 | bytes 48136 | tf_op jit(solution)/shard_map/psum | solution.py:102
  885.8 0.0 all-reduce.6.cloned.1.call-done
  885.8 1.5 copy.50
  (27 shorter events, 0.1 us)
Async XLA Ops:
  7.2 1.5 copy-start
  11.4 15.0 %copy-start.10 = (s32[256]{0:T(256)S(1)}, s32[256]{0:T(256)}, u32[]{:S(2)}) copy-start(s32[256]{0:T(256)} %param.13) | copy-start | bytes 3076
  14.6 41.2 %all-to-all-start = ((bf16[64,2,128,64]{2,3,1,0:T(8,128)(2,1)}), bf16[64,2,128,64]{2,3,1,0:T(8,128)(2,1)}, u32[]{:S(2)}, u32[]{:S(2)}) async-start(bf16[64,2,128,64]{2,3,1,0:T(8,128)(2,1)} %broadcast_select_fusion.1), calls=%async_computation | async-start | bytes 4194304 | tf_op jit(solution)/shard_map/all_to_all | solution.py:49
  26.4 88.9 %all-gather.2.cloned.1.call-start = ((), (), s32[]{:S(2)}) async-start(), calls=%async_computation.3 | async-start | bytes 3145728 | tf_op jit(solution)/shard_map/all_gather | solution.py:55
  64.3 14.0 %copy-start.9 = (s32[256]{0:T(256)S(1)}, s32[256]{0:T(256)}, u32[]{:S(2)}) copy-start(s32[256]{0:T(256)} %param.14) | copy-start | bytes 3076
  104.4 10.8 %copy-start.8 = (bf16[128,128]{1,0:T(8,128)(2,1)S(1)}, bf16[128,128]{1,0:T(8,128)(2,1)}, u32[]{:S(2)}) copy-start(bf16[128,128]{1,0:T(8,128)(2,1)} %param.9) | copy-start | bytes 98308
  105.5 209.7 %all-reduce.4.cloned.1.call-start = ((), (), s32[]{:S(2)}) async-start(), calls=%async_computation.4 | async-start | bytes 1572864 | tf_op jit(solution)/shard_map/psum | solution.py:63
  117.6 416.4 %copy-start.2 = (bf16[8192,128]{1,0:T(8,128)(2,1)}, bf16[8192,128]{1,0:T(8,128)(2,1)S(1)}, u32[]{:S(2)}) copy-start(bf16[8192,128]{1,0:T(8,128)(2,1)S(1)} %fusion) | copy-start | bytes 6291460
  285.1 4.0 copy-start.7
  285.1 30.2 %copy-start.6 = (s32[8192]{0:T(1024)S(1)}, s32[8192]{0:T(1024)}, u32[]{:S(2)}) copy-start(s32[8192]{0:T(1024)} %param.11) | copy-start | bytes 98308
  287.7 1.4 copy-start.4
  427.3 11.0 %copy-start.11 = (s32[1,64,2]{1,2,0:T(2,128)S(1)}, s32[1,64,2]{1,2,0:T(2,128)}, u32[]{:S(2)}) copy-start(s32[1,64,2]{1,2,0:T(2,128)} %param.12) | copy-start | bytes 1540
  427.3 66.0 %all-to-all-start.2 = ((bf16[64,2,128,128]{3,2,1,0:T(8,128)(2,1)}), bf16[64,2,128,128]{3,2,1,0:T(8,128)(2,1)}, u32[]{:S(2)}, u32[]{:S(2)}) async-start(bf16[64,2,128,128]{3,2,1,0:T(8,128)(2,1)} %bitcast.65), calls=%async_computation.2 | async-start | bytes 8388608 | tf_op jit(solution)/shard_map/all_to_all | solution.py:87
  438.3 447.5 %all-reduce.6.cloned.1.call-start = ((), (), s32[]{:S(2)}) async-start(), calls=%async_computation.5 | async-start | bytes 131072 | tf_op jit(solution)/shard_map/psum | solution.py:102
  533.9 1.6 copy-start.3
  535.5 2.2 copy-start.5
  535.5 351.8 %copy-start.1 = (bf16[8192,64]{0,1:T(8,128)(2,1)S(1)}, bf16[8192,64]{0,1:T(8,128)(2,1)}, u32[]{:S(2)}) copy-start(bf16[8192,64]{0,1:T(8,128)(2,1)} %param.8) | copy-start | bytes 3145732
Sparse Core Ops, SparseCore 0:
  105.7 9.5 all-gather.1
  290.9 24.3 all-reduce.3
  537.8 123.3 all-reduce.5
where the time goes:
time: 898 us; the launch traced here: 895 us
  blocking collectives  408 us (45%)
  other arithmetic  188 us (21%)
  waiting for transfers between devices  118 us (13%)
  local copies, waits for them, and re-layouts  89 us (10%)
  matrix products  52.1 us (6%)
  starting transfers between devices  22.8 us (3%)
  between operations  15.8 us (2%)
    psum x1, blocking collectives, per_device(): lax.psum((grad_first, grad_second, loss_local), 'dom')  346 us
    scatter-add x2, other arithmetic, aggregate(): summed = jax.ops.segment_sum(products, tile_dst, num_segments=NB)  78 us
    all_to_all x1, blocking collectives, per_device(): lax.all_to_all(outgoing(hidden, send_index), 'dom', split_axis=0, concat_...  62.7 us
    all_to_all x1, waiting for transfers between devices, per_device(): lax.all_to_all(partial_value[NB:].reshape(dom_count, S, BLK, half_hidden)...  54.8 us
    scatter-add x1, other arithmetic, per_device(): jax.ops.segment_sum(products, tile_src, num_segments=NB + dom_count * S)  52 us
    all_to_all x1, waiting for transfers between devices, per_device(): lax.all_to_all(outgoing(features, send_index), 'dom', split_axis=0, conca...  29.4 us
    scatter-add x1, other arithmetic, per_device(): jax.ops.segment_sum(returned.reshape(-1, BLK, half_hidden), target_block,...  26.6 us
    dot_general x2, matrix products, aggregate(): jnp.einsum('tij,tjw->tiw', tile_values, gathered, preferred_element_type=...  26.6 us
  transfers between devices with their start and end apart: 5, of which 4 were waited for; matrix products, arithmetic and copies ran while one was open for 0% of the time, Pallas kernels for 0%

commit v1 on v0

v1 whole, which is shorter than its diff:
```python
import functools

import jax
import jax.numpy as jnp
from jax import lax
from jax.experimental import pallas as pl
from jax.experimental.pallas import tpu as pltpu
from jax.sharding import PartitionSpec as P

MESH = pl.DeviceIdType.MESH
BLK = 128
NB = 64
HALF = NB // 2
S = 2
DOM = 64
NT = 256
ENTRIES = NB + DOM * S
CLS = 47
CPAD = 48
UNROLL = 4
LIST = NT + UNROLL
PAY = 192
PART = PAY // 4
VMEM_LIMIT = 48 << 20
F32 = jnp.float32
BF16 = jnp.bfloat16

VM = pl.BlockSpec(memory_space=pltpu.VMEM)
SM = pl.BlockSpec(memory_space=pltpu.SMEM)


def coords(dom):
    return dom // 16, (dom // 4) % 4, dom % 4


def shifted(dom, i, sign):
    x, z, y = coords(dom)
    dx, dz, dy = coords(i)
    return ((x + sign * dx + 4) % 4) * 16 + ((z + sign * dz + 4) % 4) * 4 + (y + sign * dy + 4) % 4


def shift_of(step):
    return (step * 22 - 1) % 63 + 1


def meet_all(dom, rep):
    barrier = pltpu.get_barrier_semaphore()

    @pl.loop(1, DOM)
    def _(i):
        pl.semaphore_signal(barrier, inc=1, device_id=(shifted(dom, i, 1), rep), device_id_type=MESH)

    pl.semaphore_signal(barrier, inc=1, device_id=(dom, 1 - rep), device_id_type=MESH)
    return lambda: pl.semaphore_wait(barrier, DOM)


def dot(a, b, dims):
    return lax.dot_general(a, b, (dims, ((), ())), preferred_element_type=F32)


NN = ((1,), (0,))
TN = ((0,), (0,))
NTR = ((1,), (1,))


def feature_kernel(pick, feat, w1, w2, table, w1_all, w2_all, outbox, inbox, other, wbox, wgot,
                   send_sem, recv_sem, fsend_sem, frecv_sem, side_send, side_recv):
    dom, rep = lax.axis_index("dom"), lax.axis_index("rep")
    sib = 1 - rep
    arrive = meet_all(dom, rep)

    @pl.loop(1, DOM)
    def _(step):
        i = shift_of(step)
        r = shifted(dom, i, 1)
        outbox[i] = jnp.concatenate([feat[pick[2 * r]], feat[pick[2 * r + 1]]], axis=1)

    w2_pad = jnp.concatenate([w2[...].astype(F32), jnp.zeros((BLK, BLK - CLS), F32)], axis=1)
    wbox[0] = w1[...]
    wbox[1] = w2_pad.T.astype(BF16)
    arrive()

    def main(i):
        return pltpu.make_async_remote_copy(
            src_ref=outbox.at[i], dst_ref=inbox.at[rep, dom], send_sem=send_sem.at[i], recv_sem=recv_sem.at[i],
            device_id=(shifted(dom, i, 1), rep), device_id_type=MESH)

    def pass_on(i):
        s = shifted(dom, i, -1)
        return pltpu.make_async_remote_copy(
            src_ref=inbox.at[rep, s], dst_ref=inbox.at[rep, s], send_sem=fsend_sem.at[i], recv_sem=frecv_sem.at[i],
            device_id=(dom, sib), device_id_type=MESH)

    def taken(i):
        s = shifted(dom, i, -1)
        return pltpu.make_async_remote_copy(
            src_ref=inbox.at[sib, s], dst_ref=inbox.at[sib, s], send_sem=fsend_sem.at[i], recv_sem=frecv_sem.at[i],
            device_id=(dom, sib), device_id_type=MESH)

    @pl.loop(1, DOM)
    def _(step):
        main(shift_of(step)).start()

    side = [
        pltpu.make_async_remote_copy(src_ref=feat, dst_ref=other, send_sem=side_send.at[0], recv_sem=side_recv.at[0],
                                     device_id=(dom, sib), device_id_type=MESH),
        pltpu.make_async_remote_copy(src_ref=wbox, dst_ref=wgot, send_sem=side_send.at[1], recv_sem=side_recv.at[1],
                                     device_id=(dom, sib), device_id_type=MESH),
    ]
    for c in side:
        c.start()
    for c in side:
        c.wait()
    w1_all[:, :BLK] = wbox[0]
    w1_all[:, BLK:] = wgot[0]
    w2_all[:, :BLK] = wbox[1][:CPAD]
    w2_all[:, BLK:] = wgot[1][:CPAD]

    @pl.loop(0, NB)
    def _(b):
        mine, yours = feat[b], other[b]
        table[b] = jnp.where(rep == 0, jnp.concatenate([mine, yours], axis=1), jnp.concatenate([yours, mine], axis=1))

    @pl.loop(1, DOM)
    def _(step):
        i = shift_of(step)
        main(i).wait_recv()
        pass_on(i).start()

    @pl.loop(1, DOM)
    def _(step):
        i = shift_of(step)
        taken(i).wait_recv()
        s = shifted(dom, i, -1)
        low, high = inbox[0, s], inbox[1, s]
        table[NB + 2 * s] = jnp.concatenate([low[:, :64], high[:, :64]], axis=1)
        table[NB + 2 * s + 1] = jnp.concatenate([low[:, 64:], high[:, 64:]], axis=1)

    @pl.loop(1, DOM)
    def _(step):
        i = shift_of(step)
        main(i).wait_send()
        pass_on(i).wait_send()


def exchange_features(pick, feat, w1, w2):
    return pl.pallas_call(
        feature_kernel,
        out_shape=(
            jax.ShapeDtypeStruct((ENTRIES, BLK, BLK), BF16),
            jax.ShapeDtypeStruct((BLK, 2 * BLK), BF16),
            jax.ShapeDtypeStruct((CPAD, 2 * BLK), BF16),
        ),
        in_specs=[SM, VM, VM, VM],
        out_specs=(VM, VM, VM),
        scratch_shapes=[
            pltpu.VMEM((DOM, BLK, BLK), BF16),
            pltpu.VMEM((2, DOM, BLK, BLK), BF16),
            pltpu.VMEM((NB, BLK, 64), BF16),
            pltpu.VMEM((2, BLK, BLK), BF16),
            pltpu.VMEM((2, BLK, BLK), BF16),
        ] + [pltpu.SemaphoreType.DMA((DOM,))] * 4 + [pltpu.SemaphoreType.DMA((2,))] * 2,
        compiler_params=pltpu.CompilerParams(collective_id=0, has_side_effects=True, vmem_limit_bytes=VMEM_LIMIT),
    )(pick, feat.reshape(NB, BLK, 64), w1, w2)


def build_list(src, dst, first, lists):
    def step(t, count):
        d = dst[t] - first
        lists[0, count] = t
        lists[1, count] = src[t]
        lists[2, count] = d
        return count + jnp.where((d >= 0) & (d < HALF), 1, 0)

    count = lax.fori_loop(NB, NT, step, 0)
    for u in range(UNROLL):
        lists[0, count + u] = 0
        lists[1, count + u] = 0
        lists[2, count + u] = HALF
    return (count + UNROLL - 1) // UNROLL


def gather_sum(groups, first, lists, tiles, table, acc):
    @pl.loop(0, HALF // UNROLL)
    def _(g):
        for u in range(UNROLL):
            b = g * UNROLL + u
            acc[b] = dot(tiles[first + b], table[first + b], NN)

    @pl.loop(0, groups)
    def _(g):
        at = [g * UNROLL + u for u in range(UNROLL)]
        products = [dot(tiles[lists[0, n]], table[lists[1, n]], NN) for n in at]
        for n, product in zip(at, products):
            acc[lists[2, n]] += product


def first_kernel(src, dst, tiles, table, mixed, acc, lists):
    first = lax.axis_index("rep") * HALF
    groups = build_list(src, dst, first, lists)
    gather_sum(groups, first, lists, tiles, table, acc)

    @pl.loop(0, HALF)
    def _(b):
        mixed[b] = acc[b].astype(BF16)


def first_aggregate(src, dst, tiles, table):
    return pl.pallas_call(
        first_kernel,
        out_shape=jax.ShapeDtypeStruct((HALF, BLK, BLK), BF16),
        in_specs=[SM, SM, VM, VM],
        out_specs=VM,
        scratch_shapes=[pltpu.VMEM((HALF + 1, BLK, BLK), F32), pltpu.SMEM((3, LIST), jnp.int32)],
        compiler_params=pltpu.CompilerParams(vmem_limit_bytes=VMEM_LIMIT),
    )(src, dst, tiles, table)


def mixed_kernel(pick, mixed, w1, table, hidden, own, outbox,
                 send_sem, recv_sem, fsend_sem, frecv_sem, side_send, side_recv):
    dom, rep = lax.axis_index("dom"), lax.axis_index("rep")
    sib = 1 - rep
    arrive = meet_all(dom, rep)

    @pl.loop(0, HALF)
    def _(b):
        own[rep * HALF + b] = mixed[b]

    arrive()
    side = pltpu.make_async_remote_copy(
        src_ref=mixed, dst_ref=own.at[pl.ds(rep * HALF, HALF)], send_sem=side_send, recv_sem=side_recv,
        device_id=(dom, sib), device_id_type=MESH)
    side.start()
    side.wait()

    def main(i):
        return pltpu.make_async_remote_copy(
            src_ref=outbox.at[i], dst_ref=table.at[NB + 2 * dom + rep], send_sem=send_sem.at[i],
            recv_sem=recv_sem.at[i], device_id=(shifted(dom, i, 1), rep), device_id_type=MESH)

    def pass_on(i):
        e = NB + 2 * shifted(dom, i, -1) + rep
        return pltpu.make_async_remote_copy(
            src_ref=table.at[e], dst_ref=table.at[e], send_sem=fsend_sem.at[i], recv_sem=frecv_sem.at[i],
            device_id=(dom, sib), device_id_type=MESH)

    def taken(i):
        e = NB + 2 * shifted(dom, i, -1) + sib
        return pltpu.make_async_remote_copy(
            src_ref=table.at[e], dst_ref=table.at[e], send_sem=fsend_sem.at[i], recv_sem=frecv_sem.at[i],
            device_id=(dom, sib), device_id_type=MESH)

    @pl.loop(1, DOM)
    def _(step):
        i = shift_of(step)
        outbox[i] = own[pick[2 * shifted(dom, i, 1) + rep]]
        main(i).start()

    def activate(e, rows):
        hidden[e] = jnp.maximum(dot(rows, w1[...], NN), 0.0).astype(BF16)

    @pl.loop(0, NB // 2)
    def _(g):
        for b in (2 * g, 2 * g + 1):
            table[b] = own[b]
            activate(b, own[b])

    @pl.loop(1, DOM)
    def _(step):
        i = shift_of(step)
        main(i).wait_recv()
        pass_on(i).start()
        e = NB + 2 * shifted(dom, i, -1) + rep
        activate(e, table[e])

    @pl.loop(1, DOM)
    def _(step):
        i = shift_of(step)
        taken(i).wait_recv()
        e = NB + 2 * shifted(dom, i, -1) + sib
        activate(e, table[e])

    @pl.loop(1, DOM)
    def _(step):
        i = shift_of(step)
        main(i).wait_send()
        pass_on(i).wait_send()


def exchange_mixed(pick, mixed, w1):
    return pl.pallas_call(
        mixed_kernel,
        out_shape=(
            jax.ShapeDtypeStruct((ENTRIES, BLK, BLK), BF16),
            jax.ShapeDtypeStruct((ENTRIES, BLK, 2 * BLK), BF16),
        ),
        in_specs=[SM, VM, VM],
        out_specs=(VM, VM),
        scratch_shapes=[pltpu.VMEM((NB, BLK, BLK), BF16), pltpu.VMEM((DOM, BLK, BLK), BF16)]
        + [pltpu.SemaphoreType.DMA((DOM,))] * 4 + [pltpu.SemaphoreType.DMA(())] * 2,
        compiler_params=pltpu.CompilerParams(collective_id=1, has_side_effects=True, vmem_limit_bytes=VMEM_LIMIT),
    )(pick, mixed, w1)


def second_kernel(scale, src, dst, labels, tiles, table, hidden, w2, pay, hidden_out, acc, grad, lists, sem):
    first = lax.axis_index("rep") * HALF
    out = pltpu.make_async_copy(hidden.at[pl.ds(0, NB), :, pl.ds(0, BLK)], hidden_out, sem)
    out.start()
    groups = build_list(src, dst, first, lists)
    gather_sum(groups, first, lists, tiles, hidden, acc)
    pay[...] = jnp.zeros_like(pay)
    grad[HALF] = jnp.zeros((BLK, 2 * BLK), BF16)
    w2_t = w2[...]
    kinds = lax.broadcasted_iota(jnp.int32, (CPAD, BLK), 0)

    def classify(b, loss):
        second = acc[b].astype(BF16)
        logits = dot(w2_t, second, NTR)
        powers = jnp.where(kinds < CLS, jnp.exp(logits), 0.0)
        total = jnp.sum(powers, axis=0, keepdims=True)
        hot = kinds == labels[b]
        loss = loss + jnp.log(total) - jnp.sum(jnp.where(hot, logits, 0.0), axis=0, keepdims=True)
        grad_logits = ((powers * (1.0 / total) - jnp.where(hot, 1.0, 0.0)) * scale).astype(BF16)
        pay[BLK:BLK + CPAD] += dot(grad_logits, second, NN)
        grad[b] = dot(grad_logits, w2_t, TN).astype(BF16)
        return loss

    def two(g, loss):
        return classify(2 * g + 1, classify(2 * g, loss))

    loss = lax.fori_loop(0, HALF // 2, two, jnp.zeros((1, BLK), F32))
    loss_sum = jnp.sum(loss)
    pay[BLK + CPAD:] = jnp.zeros((PAY - BLK - CPAD, 2 * BLK), F32) + loss_sum

    def back(t, e, d):
        part = dot(tiles[t], grad[d], TN)
        return jnp.where(hidden[e] > 0, part, 0.0).astype(BF16)

    def pair(a, b):
        rows = jnp.concatenate([table[a[1]], table[b[1]]], axis=0)
        return dot(rows, jnp.concatenate([back(*a), back(*b)], axis=0), TN)

    @pl.loop(0, HALF // UNROLL)
    def _(g):
        at = [g * UNROLL + u for u in range(UNROLL)]
        at = [(first + b, first + b, b) for b in at]
        pay[:BLK] += pair(at[0], at[1]) + pair(at[2], at[3])

    @pl.loop(0, groups)
    def _(g):
        at = [g * UNROLL + u for u in range(UNROLL)]
        at = [(lists[0, n], lists[1, n], lists[2, n]) for n in at]
        pay[:BLK] += pair(at[0], at[1]) + pair(at[2], at[3])

    out.wait()


def second_layer(scale, src, dst, labels, tiles, table, hidden, w2):
    return pl.pallas_call(
        functools.partial(second_kernel, scale),
        out_shape=(
            jax.ShapeDtypeStruct((PAY, 2 * BLK), F32),
            jax.ShapeDtypeStruct((NB, BLK, BLK), BF16),
        ),
        in_specs=[SM, SM, VM, VM, VM, VM, VM],
        out_specs=(VM, pl.BlockSpec(memory_space=pl.ANY)),
        scratch_shapes=[
            pltpu.VMEM((HALF + 1, BLK, 2 * BLK), F32),
            pltpu.VMEM((HALF + 1, BLK, 2 * BLK), BF16),
            pltpu.SMEM((3, LIST), jnp.int32),
            pltpu.SemaphoreType.DMA(()),
        ],
        compiler_params=pltpu.CompilerParams(vmem_limit_bytes=VMEM_LIMIT),
    )(src, dst, labels, tiles, table, hidden, w2)


def sum_kernel(pay, out, got, mine, parts, plane, psum, send_sem, recv_sem):
    dom, rep = lax.axis_index("dom"), lax.axis_index("rep")
    x, z, y = coords(dom)
    zy = z * 4 + y
    sib = 1 - rep

    def along_x(j):
        return ((x + j) % 4) * 16 + zy, (x + j) % 4

    def in_plane(j):
        return x * 16 + ((z + j // 4) % 4) * 4 + (y + j % 4) % 4

    barrier = pltpu.get_barrier_semaphore()
    pl.semaphore_signal(barrier, inc=1, device_id=(dom, sib), device_id_type=MESH)
    for j in range(1, 4):
        pl.semaphore_signal(barrier, inc=1, device_id=(along_x(j)[0], rep), device_id_type=MESH)
    for j in range(1, 16):
        pl.semaphore_signal(barrier, inc=1, device_id=(in_plane(j), rep), device_id_type=MESH)
    pl.semaphore_wait(barrier, 19)

    def copy(a, b, n, to):
        return pltpu.make_async_remote_copy(src_ref=a, dst_ref=b, send_sem=send_sem.at[n], recv_sem=recv_sem.at[n],
                                            device_id=to, device_id_type=MESH)

    side = copy(pay.at[:, pl.ds(BLK, BLK)], got, 0, (dom, sib))
    side.start()
    side.wait()
    mine[...] = pay[:, :BLK] + got[...]

    cut = []
    for j in range(1, 4):
        to, tx = along_x(j)
        cut.append(copy(mine.at[pl.ds(pl.multiple_of(tx * PART, 8), PART)], parts.at[j], j, (to, rep)))
        cut[-1].start()
    total = mine[pl.ds(pl.multiple_of(x * PART, 8), PART)]
    for j in range(1, 4):
        cut[j - 1].wait()
        total = total + parts[j]
    psum[...] = total

    across = []
    for j in range(1, 16):
        across.append(copy(psum, plane.at[j], 3 + j, (in_plane(j), rep)))
        across[-1].start()
    for j in range(1, 16):
        across[j - 1].wait()
    plane[0] = psum[...]
    total = plane[0]
    for j in range(1, 16):
        total = total + plane[j]
    here = pl.ds(pl.multiple_of(x * PART, 8), PART)
    out[here] = total

    back = []
    for j in range(1, 4):
        back.append(copy(out.at[here], out.at[here], 18 + j, (along_x(j)[0], rep)))
        back[-1].start()
    for c in back:
        c.wait_send()
    for j in range(1, 4):
        there = pl.ds(pl.multiple_of(((x + 4 - j) % 4) * PART, 8), PART)
        copy(out.at[there], out.at[there], 18 + j, (along_x(j)[0], rep)).wait_recv()


def sum_all(pay):
    return pl.pallas_call(
        sum_kernel,
        out_shape=jax.ShapeDtypeStruct((PAY, BLK), F32),
        in_specs=[VM],
        out_specs=VM,
        scratch_shapes=[
            pltpu.VMEM((PAY, BLK), F32),
            pltpu.VMEM((PAY, BLK), F32),
            pltpu.VMEM((4, PART, BLK), F32),
            pltpu.VMEM((16, PART, BLK), F32),
            pltpu.VMEM((PART, BLK), F32),
            pltpu.SemaphoreType.DMA((22,)),
            pltpu.SemaphoreType.DMA((22,)),
        ],
        compiler_params=pltpu.CompilerParams(collective_id=2, has_side_effects=True, vmem_limit_bytes=VMEM_LIMIT),
    )(pay)


def per_device(features, weight_first, weight_second, labels, send_index, tile_src, tile_dst, tile_values):
    node_count = lax.axis_size("dom") * NB * BLK
    pick = jnp.clip(send_index.reshape(-1), 0, NB - 1)
    table, w1, w2 = exchange_features(pick, features, weight_first, weight_second)
    mixed = first_aggregate(tile_src, tile_dst, tile_values, table)
    mixed_table, hidden = exchange_mixed(pick, mixed, w1)
    my_labels = lax.dynamic_slice(labels.reshape(NB, 1, BLK), (lax.axis_index("rep") * HALF, 0, 0), (HALF, 1, BLK))
    pay, hidden_out = second_layer(
        1.0 / node_count**0.5, tile_src, tile_dst, my_labels, tile_values, mixed_table, hidden, w2)
    total = sum_all(pay)
    grad_first = total[:BLK]
    grad_second = total[BLK:BLK + CLS].T
    loss = total[BLK + CPAD, 0] / node_count
    return hidden_out.reshape(NB * BLK, BLK), grad_first, grad_second, loss


def solution(mesh):
    return jax.shard_map(
        per_device,
        mesh=mesh,
        in_specs=(P("dom", "rep"), P(None, "rep"), P("rep", None), P("dom"), P("dom", None, None), P("dom"), P("dom"),
                  P("dom", None, None)),
        out_specs=(P("dom", "rep"), P(None, "rep"), P("rep", None), P()),
        check_vma=False,
    )
```

time: 898 us -> 202 us (0.22)
  blocking collectives: 408 us -> 0 us
  Pallas kernels: 0 us -> 191 us
  other arithmetic: 188 us -> 0.68 us
  waiting for transfers between devices: 118 us -> 0 us
  local copies, waits for them, and re-layouts: 89 us -> 7.71 us
  matrix products: 52.1 us -> 0 us
  starting transfers between devices: 22.8 us -> 0 us
  between operations: 15.8 us -> 2.5 us
    psum x1 -> x0, blocking collectives: 346 us -> none  [per_device(): lax.psum((grad_first, grad_second, loss_local), 'dom')]
    pallas_call x0 -> x5, Pallas kernels: none -> 191 us  [the longest x1 58.4 us: exchange_mixed(): pl.pallas_call(mixed_kernel, out_shape=(jax.ShapeDtypeStruct((ENTRIES, BL...]
    scatter-add x4 -> x0, other arithmetic: 157 us -> none  [the longest x2 78 us: aggregate(): summed = jax.ops.segment_sum(products, tile_dst, num_segments=NB)]
    all_to_all x2 -> x0, waiting for transfers between devices: 84.2 us -> none  [the longest x1 54.8 us: per_device(): lax.all_to_all(partial_value[NB:].reshape(dom_count, S, BLK, half_hidden)...]
    all_to_all x1 -> x0, blocking collectives: 62.7 us -> none  [per_device(): lax.all_to_all(outgoing(hidden, send_index), 'dom', split_axis=0, concat_...]
    dot_general x9 -> x0, matrix products: 52.1 us -> none  [the longest x2 26.6 us: aggregate(): jnp.einsum('tij,tjw->tiw', tile_values, gathered, preferred_element_type=...]
    dot_general x2 -> x0, local copies, waits for them, and re-layouts: 34.9 us -> none  [the longest x1 17.5 us: per_device(): jnp.einsum('tij,tiw->tjw', tile_values, grad_blocks[tile_dst], preferred_...]
    gather x5 -> x0, local copies, waits for them, and re-layouts: 31.7 us -> none  [the longest x2 16.4 us: aggregate(): gathered = block_table[tile_src]]
  transfers between devices with their start and end apart: 5 -> 0, of which waited for: 4 -> 0; matrix products, arithmetic and copies ran while one was open for 0% -> 0% of each run, Pallas kernels for 0% -> 0%
where the time goes in v1:
time: 202 us
  Pallas kernels  191 us (95%)
  local copies, waits for them, and re-layouts  7.71 us (4%)
  between operations  2.5 us (1%)
    pallas_call x1, Pallas kernels, exchange_mixed(): pl.pallas_call(mixed_kernel, out_shape=(jax.ShapeDtypeStruct((ENTRIES, BL...  58.4 us
    pallas_call x1, Pallas kernels, exchange_features(): pl.pallas_call(feature_kernel, out_shape=(jax.ShapeDtypeStruct((ENTRIES,...  53.6 us
    pallas_call x1, Pallas kernels, second_layer(): pl.pallas_call(functools.partial(second_kernel, scale), out_shape=(jax.Sh...  40.7 us
    pallas_call x1, Pallas kernels, sum_all(): pl.pallas_call(sum_kernel, out_shape=jax.ShapeDtypeStruct((PAY, BLK), F32...  25.6 us
    pallas_call x1, Pallas kernels, first_aggregate(): pl.pallas_call(first_kernel, out_shape=jax.ShapeDtypeStruct((HALF, BLK, B...  12.4 us
    unnamed x10, local copies, waits for them, and re-layouts  5.71 us

profile of v1, /device:TPU:0, one launch (start us, length us, event | category | flops | bytes accessed | tf_op | source)
XLA Modules:
  0.0 201.7 jit_solution(10346320326012975448)
XLA Ops:
  0.6 0.0 copy-start
  0.7 0.7 copy-done
  1.4 0.7 broadcast_clamp_fusion
  2.1 0.1 copy.15
  2.2 0.1 min.12.pick
  2.3 0.8 copy.17.w2
  3.1 2.0 %copy.16 = bf16[8192,64]{1,0:T(8,128)(2,1)S(1)} copy(bf16[8192,64]{0,1:T(8,128)(2,1)} %param.8) | data formatting | bytes 2097152 | tf_op args[0]
  5.2 0.0 copy-start.1
  5.2 0.7 copy-done.1
  5.9 53.6 %shard_map.111 = (bf16[192,128,128]{2,1,0:T(8,128)(2,1)}, bf16[128,256]{1,0:T(8,128)(2,1)S(1)}, bf16[48,256]{1,0:T(8,128)(2,1)S(1)}) custom-call(s32[128]{0:T(128)S(1)} %min.12.pick, bf16[64,128,64]{2,1,0:T(8,128)(2,1)S(1)} %bitcast.7, bf16[128,128]{1,0:T(8,128)(2,1)S(1)} %copy-done.1, bf16[128,47]{1,0:T(8,128)(2,1)S(1)} %copy.17.w2), custom_call_target="tpu_custom_call" | custom-call | tf_op jit(solution)/shard_map/pallas_call | solution.py:147
  59.6 0.0 copy-start.2
  59.6 0.7 copy-done.2
  60.3 0.0 copy-start.3
  60.3 0.7 copy-done.3
  60.9 12.4 %shard_map.112.mixed = bf16[32,128,128]{2,1,0:T(8,128)(2,1)S(1)} custom-call(s32[256]{0:T(256)S(1)} %copy-done.2, s32[256]{0:T(256)S(1)} %copy-done.3, bf16[256,128,128]{2,1,0:T(8,128)(2,1)} %tiles.3, bf16[192,128,128]{2,1,0:T(8,128)(2,1)} %get-tuple-element.11.table), custom_call_target="tpu_custom_call" | custom-call | tf_op jit(solution)/shard_map/pallas_call | solution.py:209
  73.3 58.4 %shard_map.113 = (bf16[192,128,128]{2,1,0:T(8,128)(2,1)}, bf16[192,128,256]{2,1,0:T(8,128)(2,1)}) custom-call(s32[128]{0:T(128)S(1)} %min.12.pick, bf16[32,128,128]{2,1,0:T(8,128)(2,1)S(1)} %shard_map.112.mixed, bf16[128,256]{1,0:T(8,128)(2,1)S(1)} %get-tuple-element.12.w1), custom_call_target="tpu_custom_call" | custom-call | tf_op jit(solution)/shard_map/pallas_call | solution.py:291
  131.8 40.7 %shard_map.114 = (f32[192,256]{1,0:T(8,128)S(1)}, bf16[64,128,128]{2,1,0:T(8,128)(2,1)}) custom-call(s32[256]{0:T(256)S(1)} %copy-done.2, s32[256]{0:T(256)S(1)} %copy-done.3, s32[32,1,128]{2,1,0:T(1,128)S(1)} %constant_dynamic-slice_fusion.labels, bf16[256,128,128]{2,1,0:T(8,128)(2,1)} %tiles.3, bf16[192,128,128]{2,1,0:T(8,128)(2,1)} %get-tuple-element.13.table, ...), custom_call_target="tpu_custom_call" | custom-call | tf_op jit(solution)/shard_map/pallas_call | solution.py:359
  172.5 25.6 %shard_map.115 = f32[192,128]{1,0:T(8,128)S(1)} custom-call(f32[192,256]{1,0:T(8,128)S(1)} %get-tuple-element.17.pay), custom_call_target="tpu_custom_call" | custom-call | tf_op jit(solution)/shard_map/pallas_call | solution.py:442
  198.1 0.5 slice.11
  199.3 0.6 slice_bitcast_fusion
  199.9 0.6 slice.9
  (1 shorter events, 0.0 us)
Async XLA Ops:
  0.6 0.8 copy-start
  5.2 0.8 copy-start.1
  59.6 0.7 copy-start.2
  60.3 0.7 copy-start.3

commit v2 on v1

v2 whole, which is shorter than its diff:
```python
import functools

import jax
import jax.numpy as jnp
from jax import lax
from jax.experimental import pallas as pl
from jax.experimental.pallas import tpu as pltpu
from jax.sharding import PartitionSpec as P

MESH = pl.DeviceIdType.MESH
BLK = 128
NB = 64
HALF = NB // 2
S = 2
DOM = 64
NT = 256
ENTRIES = NB + DOM * S
CLS = 47
CPAD = 48
UNROLL = 8
BATCH = 3
WIDE = 8
ROWS = WIDE * BLK
LIST = NT + UNROLL
PAY = 192
PART = PAY // 4
F32 = jnp.float32
BF16 = jnp.bfloat16

VM = pl.BlockSpec(memory_space=pltpu.VMEM)
SM = pl.BlockSpec(memory_space=pltpu.SMEM)
ANY = pl.BlockSpec(memory_space=pl.ANY)
COST = pl.CostEstimate(flops=10**10, bytes_accessed=10**8, transcendentals=0)


def coords(dom):
    return lax.div(dom, 16), lax.rem(lax.div(dom, 4), 4), lax.rem(dom, 4)


def shifted(dom, i, sign):
    x, z, y = coords(dom)
    dx, dz, dy = coords(i)
    return (lax.rem(x + sign * dx + 4, 4) * 16 + lax.rem(z + sign * dz + 4, 4) * 4 + lax.rem(y + sign * dy + 4, 4))


def shift_of(step):
    return lax.rem(step * 22 - 1, 63) + 1


def meet_all(dom, rep):
    barrier = pltpu.get_barrier_semaphore()
    pl.semaphore_signal(barrier, inc=1, device_id=(dom, 1 - rep), device_id_type=MESH)
    x, z, y = coords(dom)
    xs = [lax.rem(x + d, 4) * 16 for d in range(4)]
    zs = [lax.rem(z + d, 4) * 4 for d in range(4)]
    ys = [lax.rem(y + d, 4) for d in range(4)]
    for i in range(1, DOM):
        peer = xs[i // 16] + zs[i // 4 % 4] + ys[i % 4]
        pl.semaphore_signal(barrier, inc=1, device_id=(peer, rep), device_id_type=MESH)
    return lambda: pl.semaphore_wait(barrier, DOM)


def dot(a, b, dims):
    return lax.dot_general(a, b, (dims, ((), ())), preferred_element_type=F32)


NN = ((1,), (0,))
TN = ((0,), (0,))
NTR = ((1,), (1,))


def feature_kernel(pick, feat, table, blocks, outbox, send_sem, recv_sem, fsend_sem, frecv_sem, side_send, side_recv):
    dom, rep = lax.axis_index("dom"), lax.axis_index("rep")
    sib = 1 - rep
    arrive = meet_all(dom, rep)

    def half(k):
        return pl.ds(pl.multiple_of(k * 64, 64), 64)

    @pl.loop(0, NB)
    def _(b):
        blocks[b] = feat[:, pl.ds(pl.multiple_of(b * BLK, BLK), BLK)]

    @pl.loop(1, DOM)
    def _(step):
        i = shift_of(step)
        r = shifted(dom, i, 1)
        outbox[i, 0] = blocks[jnp.maximum(pick[0, r], 0)]
        outbox[i, 1] = blocks[jnp.maximum(pick[1, r], 0)]

    arrive()

    def main(i):
        return pltpu.make_async_remote_copy(
            src_ref=outbox.at[i], dst_ref=table.at[pl.ds(NB + 2 * dom, 2), half(rep)], send_sem=send_sem.at[i],
            recv_sem=recv_sem.at[i], device_id=(shifted(dom, i, 1), rep), device_id_type=MESH)

    def passed(i, k):
        part = table.at[pl.ds(NB + 2 * shifted(dom, i, -1), 2), half(k)]
        return pltpu.make_async_remote_copy(
            src_ref=part, dst_ref=part, send_sem=fsend_sem.at[i], recv_sem=frecv_sem.at[i],
            device_id=(dom, sib), device_id_type=MESH)

    @pl.loop(1, DOM)
    def _(step):
        main(shift_of(step)).start()

    @pl.loop(0, NB)
    def _(b):
        table[b, half(rep)] = blocks[b]

    def own(k):
        part = table.at[pl.ds(0, NB), half(k)]
        return pltpu.make_async_remote_copy(src_ref=part, dst_ref=part, send_sem=side_send, recv_sem=side_recv,
                                            device_id=(dom, sib), device_id_type=MESH)

    own(rep).start()

    @pl.loop(1, DOM)
    def _(step):
        i = shift_of(step)
        pltpu.make_async_remote_copy(
            src_ref=outbox.at[i], dst_ref=table.at[pl.ds(NB + 2 * shifted(dom, i, -1), 2), half(rep)],
            send_sem=send_sem.at[i], recv_sem=recv_sem.at[i], device_id=(dom, sib), device_id_type=MESH).wait_recv()
        passed(i, rep).start()

    @pl.loop(1, DOM)
    def _(i):
        main(i).wait_send()
        passed(i, rep).wait_send()
        passed(i, sib).wait_recv()

    own(rep).wait_send()
    own(sib).wait_recv()


def exchange_features(pick, feat):
    return pl.pallas_call(
        feature_kernel,
        out_shape=jax.ShapeDtypeStruct((ENTRIES, BLK, BLK), BF16),
        in_specs=[SM, VM],
        out_specs=VM,
        scratch_shapes=[
            pltpu.VMEM((NB, 64, BLK), BF16),
            pltpu.VMEM((DOM, 2, 64, BLK), BF16),
        ] + [pltpu.SemaphoreType.DMA((DOM,))] * 4 + [pltpu.SemaphoreType.DMA(())] * 2,
        cost_estimate=COST,
        compiler_params=pltpu.CompilerParams(collective_id=0, has_side_effects=True, vmem_limit_bytes=12 << 20),
    )(pick, feat)


def build_list(src, dst, first, lists):
    def step(t, count):
        d = dst[t] - first
        lists[0, count] = t
        lists[1, count] = src[t]
        lists[2, count] = d
        return count + jnp.where((d >= 0) & (d < HALF), 1, 0)

    count = lax.fori_loop(NB, NT, step, 0)
    for u in range(UNROLL):
        lists[0, count + u] = 0
        lists[1, count + u] = 0
        lists[2, count + u] = HALF
    return (count + UNROLL - 1) // UNROLL


def sum_first(first, tiles, table, acc, dims):
    @pl.loop(0, HALF // UNROLL)
    def _(g):
        for u in range(UNROLL):
            b = g * UNROLL + u
            acc[b] = dot(tiles[first + b], table[first + b], dims)


def sum_rest(groups, lists, tiles, table, acc, dims):
    @pl.loop(0, groups)
    def _(g):
        for u in range(UNROLL):
            n = g * UNROLL + u
            acc[lists[2, n]] += dot(tiles[lists[0, n]], table[lists[1, n]], dims)


def first_kernel(src_in, dst_in, tiles, table, mixed, src, dst, acc, lists, load_sem):
    first = pl.multiple_of(lax.axis_index("rep") * HALF, HALF)
    pairs = [(src_in, src), (dst_in, dst)]
    loads = [pltpu.make_async_copy(a, b, load_sem.at[n]) for n, (a, b) in enumerate(pairs)]
    for load in loads:
        load.start()
    sum_first(first, tiles, table, acc, NTR)
    for load in loads:
        load.wait()
    groups = build_list(src, dst, first, lists)
    sum_rest(groups, lists, tiles, table, acc, NTR)

    @pl.loop(0, HALF // UNROLL)
    def _(g):
        at = pl.ds(g * UNROLL, UNROLL)
        mixed[at] = acc[at].astype(BF16)


def first_aggregate(src, dst, tiles, table):
    return pl.pallas_call(
        first_kernel,
        out_shape=jax.ShapeDtypeStruct((HALF, BLK, BLK), BF16),
        in_specs=[ANY, ANY, VM, VM],
        out_specs=VM,
        scratch_shapes=[
            pltpu.SMEM((NT,), jnp.int32),
            pltpu.SMEM((NT,), jnp.int32),
            pltpu.VMEM((HALF + 1, BLK, BLK), F32),
            pltpu.SMEM((3, LIST), jnp.int32),
            pltpu.SemaphoreType.DMA((2,)),
        ],
        cost_estimate=COST,
        compiler_params=pltpu.CompilerParams(vmem_limit_bytes=14 << 20),
    )(src, dst, tiles, table)


def mixed_kernel(pick, mixed, w1, w2, table, hidden, w2_all, own, outbox, w1_all, wbox, wgot,
                 send_sem, recv_sem, fsend_sem, frecv_sem, side_send, side_recv):
    dom, rep = lax.axis_index("dom"), lax.axis_index("rep")
    sib = 1 - rep
    arrive = meet_all(dom, rep)

    @pl.loop(0, HALF)
    def _(b):
        own[rep * HALF + b] = mixed[b]

    wbox[0] = w1[...]
    wbox[1] = jnp.concatenate([w2[...].astype(F32), jnp.zeros((BLK - CLS, BLK), F32)], axis=0).astype(BF16)
    arrive()
    ends = [(mixed, own.at[pl.ds(rep * HALF, HALF)]), (wbox, wgot)]
    side = [
        pltpu.make_async_remote_copy(src_ref=a, dst_ref=b, send_sem=side_send.at[n], recv_sem=side_recv.at[n],
                                     device_id=(dom, sib), device_id_type=MESH)
        for n, (a, b) in enumerate(ends)
    ]
    for c in side:
        c.start()
    side[0].wait()

    def main(i):
        return pltpu.make_async_remote_copy(
            src_ref=outbox.at[i], dst_ref=table.at[NB + 2 * dom + rep], send_sem=send_sem.at[i],
            recv_sem=recv_sem.at[i], device_id=(shifted(dom, i, 1), rep), device_id_type=MESH)

    def pass_on(i):
        e = NB + 2 * shifted(dom, i, -1) + rep
        return pltpu.make_async_remote_copy(
            src_ref=table.at[e], dst_ref=table.at[e], send_sem=fsend_sem.at[i], recv_sem=frecv_sem.at[i],
            device_id=(dom, sib), device_id_type=MESH)

    def taken(i):
        e = NB + 2 * shifted(dom, i, -1) + sib
        return pltpu.make_async_remote_copy(
            src_ref=table.at[e], dst_ref=table.at[e], send_sem=fsend_sem.at[i], recv_sem=frecv_sem.at[i],
            device_id=(dom, sib), device_id_type=MESH)

    @pl.loop(1, DOM)
    def _(step):
        i = shift_of(step)
        outbox[i] = own[jnp.maximum(pick[rep, shifted(dom, i, 1)], 0)]
        main(i).start()

    side[1].wait()
    w1_all[:, :BLK] = wbox[0]
    w1_all[:, BLK:] = wgot[0]
    w2_all[:, :BLK] = wbox[1][:CPAD]
    w2_all[:, BLK:] = wgot[1][:CPAD]

    def activate(e, rows):
        hidden[e] = jnp.maximum(dot(rows, w1_all[...], NN), 0.0).astype(BF16)

    @pl.loop(0, NB // UNROLL)
    def _(g):
        for u in range(UNROLL):
            b = g * UNROLL + u
            rows = own[b]
            table[b] = rows
            activate(b, rows)

    def entry(i, k):
        return NB + 2 * shifted(dom, i, -1) + k

    def take(g):
        for u in range(BATCH):
            i = shift_of(g * BATCH + u + 1)
            main(i).wait_recv()
            pass_on(i).start()

    def take_passed(g):
        for u in range(BATCH):
            taken(shift_of(g * BATCH + u + 1)).wait_recv()

    def activate_batch(g, k):
        for u in range(BATCH):
            e = entry(shift_of(g * BATCH + u + 1), k)
            activate(e, table[e])

    take(0)
    activate_batch(0, rep)

    @pl.loop(1, (DOM - 1) // BATCH)
    def _(g):
        take(g)
        take_passed(g - 1)
        activate_batch(g, rep)
        activate_batch(g - 1, sib)

    take_passed((DOM - 1) // BATCH - 1)
    activate_batch((DOM - 1) // BATCH - 1, sib)

    @pl.loop(1, DOM)
    def _(i):
        main(i).wait_send()
        pass_on(i).wait_send()


def exchange_mixed(pick, mixed, w1, w2):
    return pl.pallas_call(
        mixed_kernel,
        out_shape=(
            jax.ShapeDtypeStruct((ENTRIES, BLK, BLK), BF16),
            jax.ShapeDtypeStruct((ENTRIES, BLK, 2 * BLK), BF16),
            jax.ShapeDtypeStruct((CPAD, 2 * BLK), BF16),
        ),
        in_specs=[SM, VM, VM, VM],
        out_specs=(VM, VM, VM),
        scratch_shapes=[
            pltpu.VMEM((NB, BLK, BLK), BF16),
            pltpu.VMEM((DOM, BLK, BLK), BF16),
            pltpu.VMEM((BLK, 2 * BLK), BF16),
            pltpu.VMEM((2, BLK, BLK), BF16),
            pltpu.VMEM((2, BLK, BLK), BF16),
        ] + [pltpu.SemaphoreType.DMA((DOM,))] * 4 + [pltpu.SemaphoreType.DMA((2,))] * 2,
        cost_estimate=COST,
        compiler_params=pltpu.CompilerParams(collective_id=1, has_side_effects=True, vmem_limit_bytes=12 << 20),
    )(pick, mixed, w1, w2)


def second_kernel(scale, src_in, dst_in, labels, tiles, table, hidden, w2, pay, hidden_out, src, dst, acc, grad, lists, sem,
                  load_sem):
    first = lax.axis_index("rep") * HALF
    loads = [pltpu.make_async_copy(a, b, load_sem.at[n]) for n, (a, b) in enumerate([(src_in, src), (dst_in, dst)])]
    for load in loads:
        load.start()
    out = pltpu.make_async_copy(hidden.at[pl.ds(0, NB), :, pl.ds(0, BLK)], hidden_out, sem)
    out.start()
    sum_first(first, tiles, hidden, acc, NN)
    for load in loads:
        load.wait()
    groups = build_list(src, dst, first, lists)
    sum_rest(groups, lists, tiles, hidden, acc, NN)
    pay[...] = jnp.zeros_like(pay)
    grad[HALF] = jnp.zeros((BLK, 2 * BLK), BF16)
    w2_t = w2[...]
    kinds = lax.broadcasted_iota(jnp.int32, (CPAD, ROWS), 0)

    def classify(g, loss):
        at = pl.ds(g * WIDE, WIDE)
        second = acc[at].reshape(ROWS, 2 * BLK).astype(BF16)
        logits = dot(w2_t, second, NTR)
        powers = jnp.where(kinds < CLS, jnp.exp(logits), 0.0)
        total = jnp.sum(powers, axis=0, keepdims=True)
        hot = kinds == labels[lax.axis_index("rep") * (HALF // WIDE) + g]
        loss = loss + jnp.log(total) - jnp.sum(jnp.where(hot, logits, 0.0), axis=0, keepdims=True)
        grad_logits = ((powers * (1.0 / total) - jnp.where(hot, 1.0, 0.0)) * scale).astype(BF16)
        pay[BLK:BLK + CPAD] += dot(grad_logits, second, NN)
        grad[at] = dot(grad_logits, w2_t, TN).astype(BF16).reshape(WIDE, BLK, 2 * BLK)
        return loss

    loss = lax.fori_loop(0, HALF // WIDE, classify, jnp.zeros((1, ROWS), F32))
    pay[BLK + CPAD:] = jnp.zeros((PAY - BLK - CPAD, 2 * BLK), F32) + jnp.sum(loss)

    def back(t, e, d):
        part = dot(tiles[t], grad[d], TN)
        return jnp.where(hidden[e] > 0, part, 0.0).astype(BF16)

    def pair(a, b):
        rows = jnp.concatenate([table[a[1]], table[b[1]]], axis=0)
        return dot(rows, jnp.concatenate([back(*a), back(*b)], axis=0), TN)

    def add_pairs(at):
        total = pair(at[0], at[1])
        for u in range(2, UNROLL, 2):
            total = total + pair(at[u], at[u + 1])
        pay[:BLK] += total

    @pl.loop(0, HALF // UNROLL)
    def _(g):
        at = [g * UNROLL + u for u in range(UNROLL)]
        add_pairs([(first + b, first + b, b) for b in at])

    @pl.loop(0, groups)
    def _(g):
        at = [g * UNROLL + u for u in range(UNROLL)]
        add_pairs([(lists[0, n], lists[1, n], lists[2, n]) for n in at])

    out.wait()


def second_layer(scale, src, dst, labels, tiles, table, hidden, w2):
    return pl.pallas_call(
        functools.partial(second_kernel, scale),
        out_shape=(
            jax.ShapeDtypeStruct((PAY, 2 * BLK), F32),
            jax.ShapeDtypeStruct((NB, BLK, BLK), BF16),
        ),
        in_specs=[ANY, ANY, VM, VM, VM, VM, VM],
        out_specs=(VM, ANY),
        scratch_shapes=[
            pltpu.SMEM((NT,), jnp.int32),
            pltpu.SMEM((NT,), jnp.int32),
            pltpu.VMEM((HALF + 1, BLK, 2 * BLK), F32),
            pltpu.VMEM((HALF + 1, BLK, 2 * BLK), BF16),
            pltpu.SMEM((3, LIST), jnp.int32),
            pltpu.SemaphoreType.DMA(()),
            pltpu.SemaphoreType.DMA((2,)),
        ],
        cost_estimate=COST,
        compiler_params=pltpu.CompilerParams(vmem_limit_bytes=12 << 20),
    )(src, dst, labels, tiles, table, hidden, w2)


def sum_kernel(pay, out, got, mine, parts, plane, psum, send_sem, recv_sem):
    dom, rep = lax.axis_index("dom"), lax.axis_index("rep")
    x, z, y = coords(dom)
    zy = z * 4 + y
    sib = 1 - rep

    def along_x(j):
        return ((x + j) % 4) * 16 + zy, (x + j) % 4

    def in_plane(j):
        return x * 16 + ((z + j // 4) % 4) * 4 + (y + j % 4) % 4

    barrier = pltpu.get_barrier_semaphore()
    pl.semaphore_signal(barrier, inc=1, device_id=(dom, sib), device_id_type=MESH)
    for j in range(1, 4):
        pl.semaphore_signal(barrier, inc=1, device_id=(along_x(j)[0], rep), device_id_type=MESH)
    for j in range(1, 16):
        pl.semaphore_signal(barrier, inc=1, device_id=(in_plane(j), rep), device_id_type=MESH)
    pl.semaphore_wait(barrier, 19)

    def copy(a, b, n, to):
        return pltpu.make_async_remote_copy(src_ref=a, dst_ref=b, send_sem=send_sem.at[n], recv_sem=recv_sem.at[n],
                                            device_id=to, device_id_type=MESH)

    side = copy(pay.at[:, pl.ds(BLK, BLK)], got, 0, (dom, sib))
    side.start()
    side.wait()
    mine[...] = pay[:, :BLK] + got[...]

    cut = []
    for j in range(1, 4):
        to, tx = along_x(j)
        cut.append(copy(mine.at[pl.ds(pl.multiple_of(tx * PART, 8), PART)], parts.at[j], j, (to, rep)))
        cut[-1].start()
    total = mine[pl.ds(pl.multiple_of(x * PART, 8), PART)]
    for j in range(1, 4):
        cut[j - 1].wait()
        total = total + parts[j]
    psum[...] = total

    across = []
    for j in range(1, 16):
        across.append(copy(psum, plane.at[j], 3 + j, (in_plane(j), rep)))
        across[-1].start()
    for j in range(1, 16):
        across[j - 1].wait()
    plane[0] = psum[...]
    total = plane[0]
    for j in range(1, 16):
        total = total + plane[j]
    here = pl.ds(pl.multiple_of(x * PART, 8), PART)
    out[here] = total

    back = []
    for j in range(1, 4):
        back.append(copy(out.at[here], out.at[here], 18 + j, (along_x(j)[0], rep)))
        back[-1].start()
    for c in back:
        c.wait_send()
    for j in range(1, 4):
        there = pl.ds(pl.multiple_of(((x + 4 - j) % 4) * PART, 8), PART)
        copy(out.at[there], out.at[there], 18 + j, (along_x(j)[0], rep)).wait_recv()


def sum_all(pay):
    return pl.pallas_call(
        sum_kernel,
        out_shape=jax.ShapeDtypeStruct((PAY, BLK), F32),
        in_specs=[VM],
        out_specs=VM,
        scratch_shapes=[
            pltpu.VMEM((PAY, BLK), F32),
            pltpu.VMEM((PAY, BLK), F32),
            pltpu.VMEM((4, PART, BLK), F32),
            pltpu.VMEM((16, PART, BLK), F32),
            pltpu.VMEM((PART, BLK), F32),
            pltpu.SemaphoreType.DMA((22,)),
            pltpu.SemaphoreType.DMA((22,)),
        ],
        cost_estimate=COST,
        compiler_params=pltpu.CompilerParams(collective_id=2, has_side_effects=True, vmem_limit_bytes=8 << 20),
    )(pay)


def per_device(features, weight_first, weight_second, labels, send_index, tile_src, tile_dst, tile_values):
    node_count = lax.axis_size("dom") * NB * BLK
    pick = send_index[0].T
    table = exchange_features(pick, features.T)
    mixed = first_aggregate(tile_src, tile_dst, tile_values, table)
    mixed_table, hidden, w2 = exchange_mixed(pick, mixed, weight_first, weight_second.T)
    pay, hidden_out = second_layer(
        1.0 / node_count**0.5, tile_src, tile_dst, labels.reshape(NB // WIDE, 1, ROWS), tile_values, mixed_table,
        hidden, w2)
    total = sum_all(pay)
    grad_first = total[:BLK]
    grad_second = total[BLK:BLK + CLS].T
    loss = total[BLK + CPAD, 0] / node_count
    return hidden_out.reshape(NB * BLK, BLK), grad_first, grad_second, loss


def solution(mesh):
    return jax.shard_map(
        per_device,
        mesh=mesh,
        in_specs=(P("dom", "rep"), P(None, "rep"), P("rep", None), P("dom"), P("dom", None, None), P("dom"), P("dom"),
                  P("dom", None, None)),
        out_specs=(P("dom", "rep"), P(None, "rep"), P("rep", None), P()),
        check_vma=False,
    )
```

time: 202 us -> 138 us (0.68)
  Pallas kernels: 191 us -> 131 us
  local copies, waits for them, and re-layouts: 7.71 us -> 3.69 us
    pallas_call x1, Pallas kernels: 40.7 us -> 20.6 us  [second_layer(): pl.pallas_call(functools.partial(second_kernel, scale), out_shape=(jax.Sh...]
    pallas_call x1, Pallas kernels: 58.4 us -> 42.5 us  [exchange_mixed(): pl.pallas_call(mixed_kernel, out_shape=(jax.ShapeDtypeStruct((ENTRIES, BL...]
    pallas_call x1, Pallas kernels: 53.6 us -> 39.2 us  [exchange_features(): pl.pallas_call(feature_kernel, out_shape=jax.ShapeDtypeStruct((ENTRIES, B...]
    pallas_call x1, Pallas kernels: 12.4 us -> 6.93 us  [first_aggregate(): pl.pallas_call(first_kernel, out_shape=jax.ShapeDtypeStruct((HALF, BLK, B...]
    unnamed x10 -> x18, local copies, waits for them, and re-layouts: 5.71 us -> 1.93 us
    pallas_call x1, Pallas kernels: 25.6 us -> 22.3 us  [sum_all(): pl.pallas_call(sum_kernel, out_shape=jax.ShapeDtypeStruct((PAY, BLK), F32...]
where the time goes in v2:
time: 138 us
  Pallas kernels  131 us (95%)
  local copies, waits for them, and re-layouts  3.69 us (3%)
  between operations  2.55 us (2%)
    pallas_call x1, Pallas kernels, exchange_mixed(): pl.pallas_call(mixed_kernel, out_shape=(jax.ShapeDtypeStruct((ENTRIES, BL...  42.5 us
    pallas_call x1, Pallas kernels, exchange_features(): pl.pallas_call(feature_kernel, out_shape=jax.ShapeDtypeStruct((ENTRIES, B...  39.2 us
    pallas_call x1, Pallas kernels, sum_all(): pl.pallas_call(sum_kernel, out_shape=jax.ShapeDtypeStruct((PAY, BLK), F32...  22.3 us
    pallas_call x1, Pallas kernels, second_layer(): pl.pallas_call(functools.partial(second_kernel, scale), out_shape=(jax.Sh...  20.6 us
    pallas_call x1, Pallas kernels, first_aggregate(): pl.pallas_call(first_kernel, out_shape=jax.ShapeDtypeStruct((HALF, BLK, B...  6.93 us

profile of v2, /device:TPU:0, one launch (start us, length us, event | category | flops | bytes accessed | tf_op | source)
XLA Modules:
  0.0 137.7 jit_solution(5631603940927749128)
XLA Ops:
  0.6 0.0 copy-start.1
  0.6 1.2 copy-done.1
  1.9 0.0 copy-start.5
  1.9 0.7 copy-done.5
  2.5 0.0 copy-start
  2.5 0.0 copy-start.7
  2.5 0.0 copy-start.8
  2.5 39.2 %shard_map.111.table = bf16[192,128,128]{2,1,0:T(8,128)(2,1)S(1)} custom-call(s32[2,64]{1,0:T(2,128)S(1)} %bitcast.13, bf16[64,8192]{1,0:T(8,128)(2,1)S(1)} %bitcast.10), custom_call_target="tpu_custom_call" | custom-call | flops 10000000000 | bytes 100000000 | tf_op jit(solution)/shard_map/pallas_call | solution.py:138
  41.7 0.0 copy-done
  41.7 0.0 copy-done.7
  41.7 0.0 copy-done.8
  41.7 0.0 copy-start.2
  41.8 0.0 copy-start.4
  41.8 0.0 copy-start.6
  41.8 6.9 %shard_map.112.mixed = bf16[32,128,128]{2,1,0:T(8,128)(2,1)S(1)} custom-call(s32[256]{0:T(256)S(1)} %copy-done.7, s32[256]{0:T(256)S(1)} %copy-done.8, bf16[256,128,128]{2,1,0:T(8,128)(2,1)S(1)} %copy-done, bf16[192,128,128]{2,1,0:T(8,128)(2,1)S(1)} %shard_map.111.table), custom_call_target="tpu_custom_call" | custom-call | flops 10000000000 | bytes 100000000 | tf_op jit(solution)/shard_map/pallas_call | solution.py:203
  48.7 0.0 copy-done.2
  48.7 0.0 copy-done.4
  48.7 0.0 copy-done.6
  48.7 0.0 copy-start.3
  48.8 42.5 %shard_map.113 = (bf16[192,128,128]{2,1,0:T(8,128)(2,1)S(1)}, bf16[192,128,256]{2,1,0:T(8,128)(2,1)S(1)}, bf16[48,256]{1,0:T(8,128)(2,1)S(1)}) custom-call(s32[2,64]{1,0:T(2,128)S(1)} %bitcast.14, bf16[32,128,128]{2,1,0:T(8,128)(2,1)S(1)} %shard_map.112.mixed, bf16[128,128]{1,0:T(8,128)(2,1)S(1)} %copy-done.2, bf16[47,128]{1,0:T(8,128)(2,1)S(1)} %bitcast.12), custom_call_target="tpu_custom_call" | custom-call | flops 10000000000 | bytes 100000000 | tf_op jit(solution)/shard_map/pallas_call | solution.py:321
  91.2 0.0 copy-done.3
  91.2 20.6 %shard_map.114 = (f32[192,256]{1,0:T(8,128)S(1)}, bf16[64,128,128]{2,1,0:T(8,128)(2,1)}) custom-call(s32[256]{0:T(256)S(1)} %copy-done.7, s32[256]{0:T(256)S(1)} %copy-done.8, s32[8,1,1024]{2,1,0:T(1,128)S(1)} %bitcast.11, bf16[256,128,128]{2,1,0:T(8,128)(2,1)S(1)} %copy-done, bf16[192,128,128]{2,1,0:T(8,128)(2,1)S(1)} %get-tuple-element.9.table, ...), custom_call_target="tpu_custom_call" | custom-call | flops 10000000000 | bytes 100000000 | tf_op jit(solution)/shard_map/pallas_call | solution.py:404
  111.8 22.3 %shard_map.115 = f32[192,128]{1,0:T(8,128)S(1)} custom-call(f32[192,256]{1,0:T(8,128)S(1)} %get-tuple-element.13.pay), custom_call_target="tpu_custom_call" | custom-call | flops 10000000000 | bytes 100000000 | tf_op jit(solution)/shard_map/pallas_call | solution.py:491
  134.1 0.5 slice.11
  135.3 0.6 slice_bitcast_fusion
  135.9 0.6 slice.9
Async XLA Ops:
  0.6 1.2 copy-start.1
  1.9 0.7 copy-start.5
  2.5 39.2 %copy-start = (bf16[256,128,128]{2,1,0:T(8,128)(2,1)S(1)}, bf16[256,128,128]{2,1,0:T(8,128)(2,1)}, u32[]{:S(2)}) copy-start(bf16[256,128,128]{2,1,0:T(8,128)(2,1)} %tiles.3) | copy-start | bytes 25165828
  2.5 39.2 %copy-start.7 = (s32[256]{0:T(256)S(1)}, s32[256]{0:T(256)}, u32[]{:S(2)}) copy-start(s32[256]{0:T(256)} %src_in.3) | copy-start | bytes 3076
  2.5 39.2 %copy-start.8 = (s32[256]{0:T(256)S(1)}, s32[256]{0:T(256)}, u32[]{:S(2)}) copy-start(s32[256]{0:T(256)} %dst_in.3) | copy-start | bytes 3076
  41.7 7.0 %copy-start.2 = (bf16[128,128]{1,0:T(8,128)(2,1)S(1)}, bf16[128,128]{1,0:T(8,128)(2,1)}, u32[]{:S(2)}) copy-start(bf16[128,128]{1,0:T(8,128)(2,1)} %w1.1) | copy-start | bytes 98308
  41.8 7.0 %copy-start.4 = (bf16[128,47]{0,1:T(8,128)(2,1)S(1)}, bf16[128,47]{0,1:T(8,128)(2,1)}, u32[]{:S(2)}) copy-start(bf16[128,47]{0,1:T(8,128)(2,1)} %param.10) | copy-start | bytes 36100
  41.8 7.0 %copy-start.6 = (s32[1,64,2]{1,2,0:T(2,128)S(1)}, s32[1,64,2]{1,2,0:T(2,128)}, u32[]{:S(2)}) copy-start(s32[1,64,2]{1,2,0:T(2,128)} %param.12) | copy-start | bytes 1540
  48.7 42.5 %copy-start.3 = (s32[8192]{0:T(1024)S(1)}, s32[8192]{0:T(1024)}, u32[]{:S(2)}) copy-start(s32[8192]{0:T(1024)} %param.11) | copy-start | bytes 98308

commit v3 on v2

--- a/solution.py
+++ b/solution.py
@@ -17,8 +17,9 @@
 ENTRIES = NB + DOM * S
 CLS = 47
 CPAD = 48
-UNROLL = 8
+UNROLL = 16
 BATCH = 3
+LAG = 4
 WIDE = 8
 ROWS = WIDE * BLK
 LIST = NT + UNROLL
@@ -44,7 +45,7 @@
 
 
 def shift_of(step):
-    return lax.rem(step * 22 - 1, 63) + 1
+    return lax.rem(step * 10, 63) + 1
 
 
 def meet_all(dom, rep):
@@ -116,19 +117,31 @@
 
     own(rep).start()
 
-    @pl.loop(1, DOM)
-    def _(step):
+    def take(step):
         i = shift_of(step)
         pltpu.make_async_remote_copy(
             src_ref=outbox.at[i], dst_ref=table.at[pl.ds(NB + 2 * shifted(dom, i, -1), 2), half(rep)],
             send_sem=send_sem.at[i], recv_sem=recv_sem.at[i], device_id=(dom, sib), device_id_type=MESH).wait_recv()
         passed(i, rep).start()
-
-    @pl.loop(1, DOM)
-    def _(i):
         main(i).wait_send()
+
+    def finish(step):
+        i = shift_of(step)
         passed(i, rep).wait_send()
         passed(i, sib).wait_recv()
+
+    @pl.loop(1, 1 + LAG)
+    def _(step):
+        take(step)
+
+    @pl.loop(1 + LAG, DOM)
+    def _(step):
+        take(step)
+        finish(step - LAG)
+
+    @pl.loop(DOM - LAG, DOM)
+    def _(step):
+        finish(step)
 
     own(rep).wait_send()
     own(sib).wait_recv()
@@ -157,7 +170,7 @@
         lists[2, count] = d
         return count + jnp.where((d >= 0) & (d < HALF), 1, 0)
 
-    count = lax.fori_loop(NB, NT, step, 0)
+    count = lax.fori_loop(NB, NT, step, 0, unroll=8)
     for u in range(UNROLL):
         lists[0, count + u] = 0
         lists[1, count + u] = 0
@@ -291,7 +304,10 @@
 
     def take_passed(g):
         for u in range(BATCH):
-            taken(shift_of(g * BATCH + u + 1)).wait_recv()
+            i = shift_of(g * BATCH + u + 1)
+            taken(i).wait_recv()
+            main(i).wait_send()
+            pass_on(i).wait_send()
 
     def activate_batch(g, k):
         for u in range(BATCH):
@@ -310,11 +326,6 @@
 
     take_passed((DOM - 1) // BATCH - 1)
     activate_batch((DOM - 1) // BATCH - 1, sib)
-
-    @pl.loop(1, DOM)
-    def _(i):
-        main(i).wait_send()
-        pass_on(i).wait_send()
 
 
 def exchange_mixed(pick, mixed, w1, w2):
@@ -374,28 +385,23 @@
     pay[BLK + CPAD:] = jnp.zeros((PAY - BLK - CPAD, 2 * BLK), F32) + jnp.sum(loss)
 
     def back(t, e, d):
-        part = dot(tiles[t], grad[d], TN)
-        return jnp.where(hidden[e] > 0, part, 0.0).astype(BF16)
-
-    def pair(a, b):
-        rows = jnp.concatenate([table[a[1]], table[b[1]]], axis=0)
-        return dot(rows, jnp.concatenate([back(*a), back(*b)], axis=0), TN)
-
-    def add_pairs(at):
-        total = pair(at[0], at[1])
-        for u in range(2, UNROLL, 2):
-            total = total + pair(at[u], at[u + 1])
-        pay[:BLK] += total
+        part = dot(tiles[t], grad[d], TN).astype(BF16)
+        return jnp.where(hidden[e] > 0, part, jnp.zeros_like(part))
+
+    def add_all(at):
+        masked = jnp.concatenate([back(*each) for each in at], axis=0)
+        rows = jnp.concatenate([table[each[1]] for each in at], axis=0)
+        pay[:BLK] += dot(rows, masked, TN)
 
     @pl.loop(0, HALF // UNROLL)
     def _(g):
         at = [g * UNROLL + u for u in range(UNROLL)]
-        add_pairs([(first + b, first + b, b) for b in at])
+        add_all([(first + b, first + b, b) for b in at])
 
     @pl.loop(0, groups)
     def _(g):
         at = [g * UNROLL + u for u in range(UNROLL)]
-        add_pairs([(lists[0, n], lists[1, n], lists[2, n]) for n in at])
+        add_all([(lists[0, n], lists[1, n], lists[2, n]) for n in at])
 
     out.wait()
 
@@ -423,68 +429,74 @@
     )(src, dst, labels, tiles, table, hidden, w2)
 
 
-def sum_kernel(pay, out, got, mine, parts, plane, psum, send_sem, recv_sem):
+def sum_kernel(pay, out, parts, zs, ys, first, second, send_sem, recv_sem):
     dom, rep = lax.axis_index("dom"), lax.axis_index("rep")
     x, z, y = coords(dom)
-    zy = z * 4 + y
     sib = 1 - rep
+    cores = (rep, sib)
 
     def along_x(j):
-        return ((x + j) % 4) * 16 + zy, (x + j) % 4
-
-    def in_plane(j):
-        return x * 16 + ((z + j // 4) % 4) * 4 + (y + j % 4) % 4
+        return lax.rem(x + j, 4)
+
+    def x_peer(j):
+        return along_x(j) * 16 + z * 4 + y
+
+    def z_peer(j):
+        return x * 16 + lax.rem(z + j, 4) * 4 + y
+
+    def y_peer(j):
+        return x * 16 + z * 4 + lax.rem(y + j, 4)
 
     barrier = pltpu.get_barrier_semaphore()
-    pl.semaphore_signal(barrier, inc=1, device_id=(dom, sib), device_id_type=MESH)
-    for j in range(1, 4):
-        pl.semaphore_signal(barrier, inc=1, device_id=(along_x(j)[0], rep), device_id_type=MESH)
-    for j in range(1, 16):
-        pl.semaphore_signal(barrier, inc=1, device_id=(in_plane(j), rep), device_id_type=MESH)
-    pl.semaphore_wait(barrier, 19)
+    peers = [(dom, sib)] + [(x_peer(j), c) for j in range(1, 4) for c in cores]
+    peers += [(f(j), rep) for j in range(1, 4) for f in (z_peer, y_peer)]
+    for peer in peers:
+        pl.semaphore_signal(barrier, inc=1, device_id=peer, device_id_type=MESH)
+    pl.semaphore_wait(barrier, len(peers))
 
     def copy(a, b, n, to):
         return pltpu.make_async_remote_copy(src_ref=a, dst_ref=b, send_sem=send_sem.at[n], recv_sem=recv_sem.at[n],
                                             device_id=to, device_id_type=MESH)
 
-    side = copy(pay.at[:, pl.ds(BLK, BLK)], got, 0, (dom, sib))
-    side.start()
-    side.wait()
-    mine[...] = pay[:, :BLK] + got[...]
+    def rows(k):
+        return pl.ds(pl.multiple_of(k * PART, 8), PART)
 
     cut = []
-    for j in range(1, 4):
-        to, tx = along_x(j)
-        cut.append(copy(mine.at[pl.ds(pl.multiple_of(tx * PART, 8), PART)], parts.at[j], j, (to, rep)))
-        cut[-1].start()
-    total = mine[pl.ds(pl.multiple_of(x * PART, 8), PART)]
-    for j in range(1, 4):
-        cut[j - 1].wait()
-        total = total + parts[j]
-    psum[...] = total
-
-    across = []
-    for j in range(1, 16):
-        across.append(copy(psum, plane.at[j], 3 + j, (in_plane(j), rep)))
-        across[-1].start()
-    for j in range(1, 16):
-        across[j - 1].wait()
-    plane[0] = psum[...]
-    total = plane[0]
-    for j in range(1, 16):
-        total = total + plane[j]
-    here = pl.ds(pl.multiple_of(x * PART, 8), PART)
-    out[here] = total
-
-    back = []
-    for j in range(1, 4):
-        back.append(copy(out.at[here], out.at[here], 18 + j, (along_x(j)[0], rep)))
-        back[-1].start()
+    for j in (2, 1, 3, 0):
+        for k in (1, 0):
+            if j or k:
+                cut.append(copy(pay.at[rows(along_x(j)), pl.ds(k * BLK, BLK)], parts.at[k, j], 4 * k + j,
+                                (x_peer(j), cores[k])))
+                cut[-1].start()
+    total = pay[rows(x), :BLK]
+    for c in cut:
+        c.wait()
+    for j in range(4):
+        for k in range(2):
+            if j or k:
+                total = total + parts[k, j]
+    first[...] = total
+
+    def sum_over(mine, got, n, peer):
+        sent = [copy(mine, got.at[j], n + j, (peer(j), rep)) for j in (2, 1, 3)]
+        for c in sent:
+            c.start()
+        for c in sent:
+            c.wait()
+        return mine[...] + got[1] + got[2] + got[3]
+
+    second[...] = sum_over(first, zs, 8, z_peer)
+    out[rows(x)] = sum_over(second, ys, 12, y_peer)
+
+    here = out.at[rows(x)]
+    back = [copy(here, here, 16 + j, (x_peer(j), rep)) for j in (2, 1, 3)]
+    for c in back:
+        c.start()
+    for j in (2, 1, 3):
+        there = out.at[rows(along_x(4 - j))]
+        copy(there, there, 16 + j, (x_peer(j), rep)).wait_recv()
     for c in back:
         c.wait_send()
-    for j in range(1, 4):
-        there = pl.ds(pl.multiple_of(((x + 4 - j) % 4) * PART, 8), PART)
-        copy(out.at[there], out.at[there], 18 + j, (along_x(j)[0], rep)).wait_recv()
 
 
 def sum_all(pay):
@@ -494,13 +506,13 @@
         in_specs=[VM],
         out_specs=VM,
         scratch_shapes=[
-            pltpu.VMEM((PAY, BLK), F32),
-            pltpu.VMEM((PAY, BLK), F32),
+            pltpu.VMEM((2, 4, PART, BLK), F32),
             pltpu.VMEM((4, PART, BLK), F32),
-            pltpu.VMEM((16, PART, BLK), F32),
+            pltpu.VMEM((4, PART, BLK), F32),
             pltpu.VMEM((PART, BLK), F32),
-            pltpu.SemaphoreType.DMA((22,)),
-            pltpu.SemaphoreType.DMA((22,)),
+            pltpu.VMEM((PART, BLK), F32),
+            pltpu.SemaphoreType.DMA((20,)),
+            pltpu.SemaphoreType.DMA((20,)),
         ],
         cost_estimate=COST,
         compiler_params=pltpu.CompilerParams(collective_id=2, has_side_effects=True, vmem_limit_bytes=8 << 20),

time: 138 us -> 127 us (0.920)
  Pallas kernels: 131 us -> 121 us
    pallas_call x1, Pallas kernels: 20.6 us -> 13.6 us  [second_layer(): pl.pallas_call(functools.partial(second_kernel, scale), out_shape=(jax.Sh...]
    pallas_call x1, Pallas kernels: 6.93 us -> 5.23 us  [first_aggregate(): pl.pallas_call(first_kernel, out_shape=jax.ShapeDtypeStruct((HALF, BLK, B...]
    pallas_call x1, Pallas kernels: 22.3 us -> 20.6 us  [sum_all(): pl.pallas_call(sum_kernel, out_shape=jax.ShapeDtypeStruct((PAY, BLK), F32...]
where the time goes in v3:
time: 127 us
  Pallas kernels  121 us (95%)
  local copies, waits for them, and re-layouts  3.69 us (3%)
  between operations  2.55 us (2%)
    pallas_call x1, Pallas kernels, exchange_mixed(): pl.pallas_call(mixed_kernel, out_shape=(jax.ShapeDtypeStruct((ENTRIES, BL...  42.3 us
    pallas_call x1, Pallas kernels, exchange_features(): pl.pallas_call(feature_kernel, out_shape=jax.ShapeDtypeStruct((ENTRIES, B...  39.1 us
    pallas_call x1, Pallas kernels, sum_all(): pl.pallas_call(sum_kernel, out_shape=jax.ShapeDtypeStruct((PAY, BLK), F32...  20.6 us
    pallas_call x1, Pallas kernels, second_layer(): pl.pallas_call(functools.partial(second_kernel, scale), out_shape=(jax.Sh...  13.6 us
    pallas_call x1, Pallas kernels, first_aggregate(): pl.pallas_call(first_kernel, out_shape=jax.ShapeDtypeStruct((HALF, BLK, B...  5.23 us

profile of v3, /device:TPU:0, one launch (start us, length us, event | category | flops | bytes accessed | tf_op | source)
XLA Modules:
  0.0 127.1 jit_solution(13495292066330295073)
XLA Ops:
  0.6 0.0 copy-start.1
  0.6 1.2 copy-done.1
  1.9 0.0 copy-start.5
  1.9 0.7 copy-done.5
  2.5 0.0 copy-start
  2.5 0.0 copy-start.7
  2.5 0.0 copy-start.8
  2.5 39.1 %shard_map.111.table = bf16[192,128,128]{2,1,0:T(8,128)(2,1)S(1)} custom-call(s32[2,64]{1,0:T(2,128)S(1)} %bitcast.13, bf16[64,8192]{1,0:T(8,128)(2,1)S(1)} %bitcast.10), custom_call_target="tpu_custom_call" | custom-call | flops 10000000000 | bytes 100000000 | tf_op jit(solution)/shard_map/pallas_call | solution.py:151
  41.6 0.0 copy-done
  41.7 0.0 copy-done.7
  41.7 0.0 copy-done.8
  41.7 0.0 copy-start.2
  41.7 0.0 copy-start.4
  41.7 0.0 copy-start.6
  41.7 5.2 %shard_map.112.mixed = bf16[32,128,128]{2,1,0:T(8,128)(2,1)S(1)} custom-call(s32[256]{0:T(256)S(1)} %copy-done.7, s32[256]{0:T(256)S(1)} %copy-done.8, bf16[256,128,128]{2,1,0:T(8,128)(2,1)S(1)} %copy-done, bf16[192,128,128]{2,1,0:T(8,128)(2,1)S(1)} %shard_map.111.table), custom_call_target="tpu_custom_call" | custom-call | flops 10000000000 | bytes 100000000 | tf_op jit(solution)/shard_map/pallas_call | solution.py:216
  47.0 0.0 copy-done.2
  47.0 0.0 copy-done.4
  47.0 0.0 copy-done.6
  47.0 0.0 copy-start.3
  47.0 42.3 %shard_map.113 = (bf16[192,128,128]{2,1,0:T(8,128)(2,1)S(1)}, bf16[192,128,256]{2,1,0:T(8,128)(2,1)S(1)}, bf16[48,256]{1,0:T(8,128)(2,1)S(1)}) custom-call(s32[2,64]{1,0:T(2,128)S(1)} %bitcast.14, bf16[32,128,128]{2,1,0:T(8,128)(2,1)S(1)} %shard_map.112.mixed, bf16[128,128]{1,0:T(8,128)(2,1)S(1)} %copy-done.2, bf16[47,128]{1,0:T(8,128)(2,1)S(1)} %bitcast.12), custom_call_target="tpu_custom_call" | custom-call | flops 10000000000 | bytes 100000000 | tf_op jit(solution)/shard_map/pallas_call | solution.py:332
  89.3 0.0 copy-done.3
  89.3 13.6 %shard_map.114 = (f32[192,256]{1,0:T(8,128)S(1)}, bf16[64,128,128]{2,1,0:T(8,128)(2,1)}) custom-call(s32[256]{0:T(256)S(1)} %copy-done.7, s32[256]{0:T(256)S(1)} %copy-done.8, s32[8,1,1024]{2,1,0:T(1,128)S(1)} %bitcast.11, bf16[256,128,128]{2,1,0:T(8,128)(2,1)S(1)} %copy-done, bf16[192,128,128]{2,1,0:T(8,128)(2,1)S(1)} %get-tuple-element.9.table, ...), custom_call_target="tpu_custom_call" | custom-call | flops 10000000000 | bytes 100000000 | tf_op jit(solution)/shard_map/pallas_call | solution.py:410
  103.0 20.6 %shard_map.115 = f32[192,128]{1,0:T(8,128)S(1)} custom-call(f32[192,256]{1,0:T(8,128)S(1)} %get-tuple-element.13.pay), custom_call_target="tpu_custom_call" | custom-call | flops 10000000000 | bytes 100000000 | tf_op jit(solution)/shard_map/pallas_call | solution.py:503
  123.6 0.5 slice.11
  124.7 0.6 slice_bitcast_fusion
  125.4 0.6 slice.9
Async XLA Ops:
  0.6 1.2 copy-start.1
  1.9 0.7 copy-start.5
  2.5 39.1 %copy-start = (bf16[256,128,128]{2,1,0:T(8,128)(2,1)S(1)}, bf16[256,128,128]{2,1,0:T(8,128)(2,1)}, u32[]{:S(2)}) copy-start(bf16[256,128,128]{2,1,0:T(8,128)(2,1)} %tiles.3) | copy-start | bytes 25165828
  2.5 39.1 %copy-start.7 = (s32[256]{0:T(256)S(1)}, s32[256]{0:T(256)}, u32[]{:S(2)}) copy-start(s32[256]{0:T(256)} %src_in.3) | copy-start | bytes 3076
  2.5 39.1 %copy-start.8 = (s32[256]{0:T(256)S(1)}, s32[256]{0:T(256)}, u32[]{:S(2)}) copy-start(s32[256]{0:T(256)} %dst_in.3) | copy-start | bytes 3076
  41.7 5.3 %copy-start.2 = (bf16[128,128]{1,0:T(8,128)(2,1)S(1)}, bf16[128,128]{1,0:T(8,128)(2,1)}, u32[]{:S(2)}) copy-start(bf16[128,128]{1,0:T(8,128)(2,1)} %w1.1) | copy-start | bytes 98308
  41.7 5.3 %copy-start.4 = (bf16[128,47]{0,1:T(8,128)(2,1)S(1)}, bf16[128,47]{0,1:T(8,128)(2,1)}, u32[]{:S(2)}) copy-start(bf16[128,47]{0,1:T(8,128)(2,1)} %param.10) | copy-start | bytes 36100
  41.7 5.3 %copy-start.6 = (s32[1,64,2]{1,2,0:T(2,128)S(1)}, s32[1,64,2]{1,2,0:T(2,128)}, u32[]{:S(2)}) copy-start(s32[1,64,2]{1,2,0:T(2,128)} %param.12) | copy-start | bytes 1540
  47.0 42.3 %copy-start.3 = (s32[8192]{0:T(1024)S(1)}, s32[8192]{0:T(1024)}, u32[]{:S(2)}) copy-start(s32[8192]{0:T(1024)} %param.11) | copy-start | bytes 98308

commit v4 on v3

--- a/solution.py
+++ b/solution.py
@@ -19,7 +19,7 @@
 CPAD = 48
 UNROLL = 16
 BATCH = 3
-LAG = 4
+MANY = 32
 WIDE = 8
 ROWS = WIDE * BLK
 LIST = NT + UNROLL
@@ -48,17 +48,22 @@
     return lax.rem(step * 10, 63) + 1
 
 
-def meet_all(dom, rep):
+def hops(i):
+    return sum(min(d, 4 - d) for d in (i // 16, i // 4 % 4, i % 4))
+
+
+def meet_all(dom, rep, sibling):
     barrier = pltpu.get_barrier_semaphore()
-    pl.semaphore_signal(barrier, inc=1, device_id=(dom, 1 - rep), device_id_type=MESH)
     x, z, y = coords(dom)
     xs = [lax.rem(x + d, 4) * 16 for d in range(4)]
     zs = [lax.rem(z + d, 4) * 4 for d in range(4)]
     ys = [lax.rem(y + d, 4) for d in range(4)]
-    for i in range(1, DOM):
+    for i in sorted(range(1, DOM), key=lambda i: -hops(i)):
         peer = xs[i // 16] + zs[i // 4 % 4] + ys[i % 4]
         pl.semaphore_signal(barrier, inc=1, device_id=(peer, rep), device_id_type=MESH)
-    return lambda: pl.semaphore_wait(barrier, DOM)
+    if sibling:
+        pl.semaphore_signal(barrier, inc=1, device_id=(dom, 1 - rep), device_id_type=MESH)
+    return lambda: pl.semaphore_wait(barrier, DOM if sibling else DOM - 1)
 
 
 def dot(a, b, dims):
@@ -70,18 +75,13 @@
 NTR = ((1,), (1,))
 
 
-def feature_kernel(pick, feat, table, blocks, outbox, send_sem, recv_sem, fsend_sem, frecv_sem, side_send, side_recv):
-    dom, rep = lax.axis_index("dom"), lax.axis_index("rep")
-    sib = 1 - rep
-    arrive = meet_all(dom, rep)
-
-    def half(k):
-        return pl.ds(pl.multiple_of(k * 64, 64), 64)
-
-    @pl.loop(0, NB)
-    def _(b):
-        blocks[b] = feat[:, pl.ds(pl.multiple_of(b * BLK, BLK), BLK)]
-
+def send_copy(dom, rep, i, outbox, landing, send_sem, recv_sem):
+    return pltpu.make_async_remote_copy(
+        src_ref=outbox.at[i], dst_ref=landing, send_sem=send_sem.at[i], recv_sem=recv_sem.at[i],
+        device_id=(shifted(dom, i, 1), rep), device_id_type=MESH)
+
+
+def pack(dom, pick, blocks, outbox):
     @pl.loop(1, DOM)
     def _(step):
         i = shift_of(step)
@@ -89,140 +89,88 @@
         outbox[i, 0] = blocks[jnp.maximum(pick[0, r], 0)]
         outbox[i, 1] = blocks[jnp.maximum(pick[1, r], 0)]
 
+
+def feature_kernel(pick, feat, table, blocks, outbox, send_sem, recv_sem):
+    dom, rep = lax.axis_index("dom"), lax.axis_index("rep")
+    arrive = meet_all(dom, rep, False)
+
+    @pl.loop(0, NB)
+    def _(b):
+        blocks[b] = feat[:, pl.ds(pl.multiple_of(b * BLK, BLK), BLK)]
+
+    pack(dom, pick, blocks, outbox)
     arrive()
 
-    def main(i):
-        return pltpu.make_async_remote_copy(
-            src_ref=outbox.at[i], dst_ref=table.at[pl.ds(NB + 2 * dom, 2), half(rep)], send_sem=send_sem.at[i],
-            recv_sem=recv_sem.at[i], device_id=(shifted(dom, i, 1), rep), device_id_type=MESH)
-
-    def passed(i, k):
-        part = table.at[pl.ds(NB + 2 * shifted(dom, i, -1), 2), half(k)]
-        return pltpu.make_async_remote_copy(
-            src_ref=part, dst_ref=part, send_sem=fsend_sem.at[i], recv_sem=frecv_sem.at[i],
-            device_id=(dom, sib), device_id_type=MESH)
+    def main(i, s):
+        return send_copy(dom, rep, i, outbox, table.at[pl.ds(NB + 2 * s, 2)], send_sem, recv_sem)
 
     @pl.loop(1, DOM)
     def _(step):
-        main(shift_of(step)).start()
+        main(shift_of(step), dom).start()
 
     @pl.loop(0, NB)
     def _(b):
-        table[b, half(rep)] = blocks[b]
-
-    def own(k):
-        part = table.at[pl.ds(0, NB), half(k)]
-        return pltpu.make_async_remote_copy(src_ref=part, dst_ref=part, send_sem=side_send, recv_sem=side_recv,
-                                            device_id=(dom, sib), device_id_type=MESH)
-
-    own(rep).start()
-
-    def take(step):
+        table[b] = blocks[b]
+
+    @pl.loop(1, DOM)
+    def _(step):
         i = shift_of(step)
-        pltpu.make_async_remote_copy(
-            src_ref=outbox.at[i], dst_ref=table.at[pl.ds(NB + 2 * shifted(dom, i, -1), 2), half(rep)],
-            send_sem=send_sem.at[i], recv_sem=recv_sem.at[i], device_id=(dom, sib), device_id_type=MESH).wait_recv()
-        passed(i, rep).start()
-        main(i).wait_send()
-
-    def finish(step):
-        i = shift_of(step)
-        passed(i, rep).wait_send()
-        passed(i, sib).wait_recv()
-
-    @pl.loop(1, 1 + LAG)
-    def _(step):
-        take(step)
-
-    @pl.loop(1 + LAG, DOM)
-    def _(step):
-        take(step)
-        finish(step - LAG)
-
-    @pl.loop(DOM - LAG, DOM)
-    def _(step):
-        finish(step)
-
-    own(rep).wait_send()
-    own(sib).wait_recv()
+        main(i, shifted(dom, i, -1)).wait_recv()
+        main(i, dom).wait_send()
 
 
 def exchange_features(pick, feat):
     return pl.pallas_call(
         feature_kernel,
-        out_shape=jax.ShapeDtypeStruct((ENTRIES, BLK, BLK), BF16),
+        out_shape=jax.ShapeDtypeStruct((ENTRIES, 64, BLK), BF16),
         in_specs=[SM, VM],
         out_specs=VM,
         scratch_shapes=[
             pltpu.VMEM((NB, 64, BLK), BF16),
             pltpu.VMEM((DOM, 2, 64, BLK), BF16),
-        ] + [pltpu.SemaphoreType.DMA((DOM,))] * 4 + [pltpu.SemaphoreType.DMA(())] * 2,
+        ] + [pltpu.SemaphoreType.DMA((DOM,))] * 2,
         cost_estimate=COST,
         compiler_params=pltpu.CompilerParams(collective_id=0, has_side_effects=True, vmem_limit_bytes=12 << 20),
     )(pick, feat)
 
 
-def build_list(src, dst, first, lists):
-    def step(t, count):
-        d = dst[t] - first
-        lists[0, count] = t
-        lists[1, count] = src[t]
-        lists[2, count] = d
-        return count + jnp.where((d >= 0) & (d < HALF), 1, 0)
-
-    count = lax.fori_loop(NB, NT, step, 0, unroll=8)
-    for u in range(UNROLL):
-        lists[0, count + u] = 0
-        lists[1, count + u] = 0
-        lists[2, count + u] = HALF
-    return (count + UNROLL - 1) // UNROLL
-
-
-def sum_first(first, tiles, table, acc, dims):
-    @pl.loop(0, HALF // UNROLL)
-    def _(g):
-        for u in range(UNROLL):
-            b = g * UNROLL + u
-            acc[b] = dot(tiles[first + b], table[first + b], dims)
-
-
-def sum_rest(groups, lists, tiles, table, acc, dims):
-    @pl.loop(0, groups)
-    def _(g):
-        for u in range(UNROLL):
-            n = g * UNROLL + u
-            acc[lists[2, n]] += dot(tiles[lists[0, n]], table[lists[1, n]], dims)
-
-
-def first_kernel(src_in, dst_in, tiles, table, mixed, src, dst, acc, lists, load_sem):
-    first = pl.multiple_of(lax.axis_index("rep") * HALF, HALF)
+def first_kernel(src_in, dst_in, tiles, table, mixed, src, dst, acc, load_sem):
     pairs = [(src_in, src), (dst_in, dst)]
     loads = [pltpu.make_async_copy(a, b, load_sem.at[n]) for n, (a, b) in enumerate(pairs)]
     for load in loads:
         load.start()
-    sum_first(first, tiles, table, acc, NTR)
+
+    @pl.loop(0, NB // MANY)
+    def _(g):
+        for u in range(MANY):
+            b = g * MANY + u
+            acc[b] = dot(table[b], tiles[b], NTR)
+
     for load in loads:
         load.wait()
-    groups = build_list(src, dst, first, lists)
-    sum_rest(groups, lists, tiles, table, acc, NTR)
-
-    @pl.loop(0, HALF // UNROLL)
-    def _(g):
-        at = pl.ds(g * UNROLL, UNROLL)
+
+    @pl.loop(NB // MANY, NT // MANY)
+    def _(g):
+        for u in range(MANY):
+            t = g * MANY + u
+            acc[dst[t]] += dot(table[src[t]], tiles[t], NTR)
+
+    @pl.loop(0, NB // MANY)
+    def _(g):
+        at = pl.ds(g * MANY, MANY)
         mixed[at] = acc[at].astype(BF16)
 
 
 def first_aggregate(src, dst, tiles, table):
     return pl.pallas_call(
         first_kernel,
-        out_shape=jax.ShapeDtypeStruct((HALF, BLK, BLK), BF16),
+        out_shape=jax.ShapeDtypeStruct((NB, 64, BLK), BF16),
         in_specs=[ANY, ANY, VM, VM],
         out_specs=VM,
         scratch_shapes=[
             pltpu.SMEM((NT,), jnp.int32),
             pltpu.SMEM((NT,), jnp.int32),
-            pltpu.VMEM((HALF + 1, BLK, BLK), F32),
-            pltpu.SMEM((3, LIST), jnp.int32),
+            pltpu.VMEM((NB, 64, BLK), F32),
             pltpu.SemaphoreType.DMA((2,)),
         ],
         cost_estimate=COST,
@@ -230,102 +178,84 @@
     )(src, dst, tiles, table)
 
 
-def mixed_kernel(pick, mixed, w1, w2, table, hidden, w2_all, own, outbox, w1_all, wbox, wgot,
+def mixed_kernel(pick, mixed, w1, w2, table, hidden, w2_all, outbox, w1_all, wbox, wgot,
                  send_sem, recv_sem, fsend_sem, frecv_sem, side_send, side_recv):
     dom, rep = lax.axis_index("dom"), lax.axis_index("rep")
     sib = 1 - rep
-    arrive = meet_all(dom, rep)
-
-    @pl.loop(0, HALF)
-    def _(b):
-        own[rep * HALF + b] = mixed[b]
-
+    arrive = meet_all(dom, rep, True)
+    pack(dom, pick, mixed, outbox)
     wbox[0] = w1[...]
     wbox[1] = jnp.concatenate([w2[...].astype(F32), jnp.zeros((BLK - CLS, BLK), F32)], axis=0).astype(BF16)
     arrive()
-    ends = [(mixed, own.at[pl.ds(rep * HALF, HALF)]), (wbox, wgot)]
-    side = [
-        pltpu.make_async_remote_copy(src_ref=a, dst_ref=b, send_sem=side_send.at[n], recv_sem=side_recv.at[n],
-                                     device_id=(dom, sib), device_id_type=MESH)
-        for n, (a, b) in enumerate(ends)
-    ]
-    for c in side:
-        c.start()
-    side[0].wait()
-
-    def main(i):
-        return pltpu.make_async_remote_copy(
-            src_ref=outbox.at[i], dst_ref=table.at[NB + 2 * dom + rep], send_sem=send_sem.at[i],
-            recv_sem=recv_sem.at[i], device_id=(shifted(dom, i, 1), rep), device_id_type=MESH)
-
-    def pass_on(i):
-        e = NB + 2 * shifted(dom, i, -1) + rep
-        return pltpu.make_async_remote_copy(
-            src_ref=table.at[e], dst_ref=table.at[e], send_sem=fsend_sem.at[i], recv_sem=frecv_sem.at[i],
-            device_id=(dom, sib), device_id_type=MESH)
-
-    def taken(i):
-        e = NB + 2 * shifted(dom, i, -1) + sib
-        return pltpu.make_async_remote_copy(
-            src_ref=table.at[e], dst_ref=table.at[e], send_sem=fsend_sem.at[i], recv_sem=frecv_sem.at[i],
-            device_id=(dom, sib), device_id_type=MESH)
+
+    def half(k):
+        return pl.ds(pl.multiple_of(k * 64, 64), 64)
+
+    def main(i, s):
+        return send_copy(dom, rep, i, outbox, table.at[pl.ds(NB + 2 * s, 2), half(rep)], send_sem, recv_sem)
+
+    def to_sibling(a, b, send, recv):
+        return pltpu.make_async_remote_copy(src_ref=a, dst_ref=b, send_sem=send, recv_sem=recv,
+                                            device_id=(dom, sib), device_id_type=MESH)
+
+    def passed(i, k):
+        part = table.at[pl.ds(NB + 2 * shifted(dom, i, -1), 2), half(k)]
+        return to_sibling(part, part, fsend_sem.at[i], frecv_sem.at[i])
 
     @pl.loop(1, DOM)
     def _(step):
-        i = shift_of(step)
-        outbox[i] = own[jnp.maximum(pick[rep, shifted(dom, i, 1)], 0)]
-        main(i).start()
-
-    side[1].wait()
+        main(shift_of(step), dom).start()
+
+    weights = to_sibling(wbox, wgot, side_send.at[0], side_recv.at[0])
+    own = to_sibling(mixed, table.at[pl.ds(0, NB), half(rep)], side_send.at[1], side_recv.at[1])
+    weights.start()
+    own.start()
+
+    @pl.loop(0, NB)
+    def _(b):
+        table[b, half(rep)] = mixed[b]
+
+    weights.wait()
     w1_all[:, :BLK] = wbox[0]
     w1_all[:, BLK:] = wgot[0]
     w2_all[:, :BLK] = wbox[1][:CPAD]
     w2_all[:, BLK:] = wgot[1][:CPAD]
-
-    def activate(e, rows):
-        hidden[e] = jnp.maximum(dot(rows, w1_all[...], NN), 0.0).astype(BF16)
+    own.wait_send()
+    to_sibling(mixed, table.at[pl.ds(0, NB), half(sib)], side_send.at[1], side_recv.at[1]).wait_recv()
+
+    def activate(e):
+        hidden[e] = jnp.maximum(dot(table[e], w1_all[...], TN), 0.0).astype(BF16)
 
     @pl.loop(0, NB // UNROLL)
     def _(g):
         for u in range(UNROLL):
-            b = g * UNROLL + u
-            rows = own[b]
-            table[b] = rows
-            activate(b, rows)
-
-    def entry(i, k):
-        return NB + 2 * shifted(dom, i, -1) + k
+            activate(g * UNROLL + u)
 
     def take(g):
         for u in range(BATCH):
             i = shift_of(g * BATCH + u + 1)
-            main(i).wait_recv()
-            pass_on(i).start()
-
-    def take_passed(g):
-        for u in range(BATCH):
-            i = shift_of(g * BATCH + u + 1)
-            taken(i).wait_recv()
-            main(i).wait_send()
-            pass_on(i).wait_send()
-
-    def activate_batch(g, k):
-        for u in range(BATCH):
-            e = entry(shift_of(g * BATCH + u + 1), k)
-            activate(e, table[e])
+            main(i, shifted(dom, i, -1)).wait_recv()
+            passed(i, rep).start()
+
+    def finish(g):
+        shifts = [shift_of(g * BATCH + u + 1) for u in range(BATCH)]
+        for i in shifts:
+            main(i, dom).wait_send()
+            passed(i, rep).wait_send()
+            passed(i, sib).wait_recv()
+        for i in shifts:
+            e = NB + 2 * shifted(dom, i, -1)
+            activate(e)
+            activate(e + 1)
 
     take(0)
-    activate_batch(0, rep)
 
     @pl.loop(1, (DOM - 1) // BATCH)
     def _(g):
         take(g)
-        take_passed(g - 1)
-        activate_batch(g, rep)
-        activate_batch(g - 1, sib)
-
-    take_passed((DOM - 1) // BATCH - 1)
-    activate_batch((DOM - 1) // BATCH - 1, sib)
+        finish(g - 1)
+
+    finish((DOM - 1) // BATCH - 1)
 
 
 def exchange_mixed(pick, mixed, w1, w2):
@@ -339,8 +269,7 @@
         in_specs=[SM, VM, VM, VM],
         out_specs=(VM, VM, VM),
         scratch_shapes=[
-            pltpu.VMEM((NB, BLK, BLK), BF16),
-            pltpu.VMEM((DOM, BLK, BLK), BF16),
+            pltpu.VMEM((DOM, 2, 64, BLK), BF16),
             pltpu.VMEM((BLK, 2 * BLK), BF16),
             pltpu.VMEM((2, BLK, BLK), BF16),
             pltpu.VMEM((2, BLK, BLK), BF16),
@@ -348,6 +277,38 @@
         cost_estimate=COST,
         compiler_params=pltpu.CompilerParams(collective_id=1, has_side_effects=True, vmem_limit_bytes=12 << 20),
     )(pick, mixed, w1, w2)
+
+
+def build_list(src, dst, first, lists):
+    def step(t, count):
+        d = dst[t] - first
+        lists[0, count] = t
+        lists[1, count] = src[t]
+        lists[2, count] = d
+        return count + jnp.where((d >= 0) & (d < HALF), 1, 0)
+
+    count = lax.fori_loop(NB, NT, step, 0, unroll=8)
+    for u in range(UNROLL):
+        lists[0, count + u] = 0
+        lists[1, count + u] = 0
+        lists[2, count + u] = HALF
+    return (count + UNROLL - 1) // UNROLL
+
+
+def sum_first(first, tiles, table, acc, dims):
+    @pl.loop(0, HALF // UNROLL)
+    def _(g):
+        for u in range(UNROLL):
+            b = g * UNROLL + u
+            acc[b] = dot(tiles[first + b], table[first + b], dims)
+
+
+def sum_rest(groups, lists, tiles, table, acc, dims):
+    @pl.loop(0, groups)
+    def _(g):
+        for u in range(UNROLL):
+            n = g * UNROLL + u
+            acc[lists[2, n]] += dot(tiles[lists[0, n]], table[lists[1, n]], dims)
 
 
 def second_kernel(scale, src_in, dst_in, labels, tiles, table, hidden, w2, pay, hidden_out, src, dst, acc, grad, lists, sem,
@@ -390,8 +351,8 @@
 
     def add_all(at):
         masked = jnp.concatenate([back(*each) for each in at], axis=0)
-        rows = jnp.concatenate([table[each[1]] for each in at], axis=0)
-        pay[:BLK] += dot(rows, masked, TN)
+        rows = jnp.concatenate([table[each[1]] for each in at], axis=1)
+        pay[:BLK] += dot(rows, masked, NN)
 
     @pl.loop(0, HALF // UNROLL)
     def _(g):
@@ -529,10 +490,8 @@
         1.0 / node_count**0.5, tile_src, tile_dst, labels.reshape(NB // WIDE, 1, ROWS), tile_values, mixed_table,
         hidden, w2)
     total = sum_all(pay)
-    grad_first = total[:BLK]
-    grad_second = total[BLK:BLK + CLS].T
     loss = total[BLK + CPAD, 0] / node_count
-    return hidden_out.reshape(NB * BLK, BLK), grad_first, grad_second, loss
+    return hidden_out.reshape(NB * BLK, BLK), total[:BLK], total[BLK:BLK + CLS].T, loss
 
 
 def solution(mesh):

time: 127 us -> 121 us (0.953)
  Pallas kernels: 121 us -> 114 us
    pallas_call x1, Pallas kernels: 42.3 us -> 36.1 us  [exchange_mixed(): pl.pallas_call(mixed_kernel, out_shape=(jax.ShapeDtypeStruct((ENTRIES, BL...]
    pallas_call x2, Pallas kernels: 44.3 us -> 43 us  [the longest x1 36.3 us: exchange_features(): pl.pallas_call(feature_kernel, out_shape=jax.ShapeDtypeStruct((ENTRIES, 6...]
where the time goes in v4:
time: 121 us; the launch traced here: 120 us
  Pallas kernels  114 us (94%)
  local copies, waits for them, and re-layouts  3.69 us (3%)
  between operations  2.55 us (2%)
    pallas_call x1, Pallas kernels, exchange_features(): pl.pallas_call(feature_kernel, out_shape=jax.ShapeDtypeStruct((ENTRIES, 6...  36.3 us
    pallas_call x1, Pallas kernels, exchange_mixed(): pl.pallas_call(mixed_kernel, out_shape=(jax.ShapeDtypeStruct((ENTRIES, BL...  36.1 us
    pallas_call x1, Pallas kernels, sum_all(): pl.pallas_call(sum_kernel, out_shape=jax.ShapeDtypeStruct((PAY, BLK), F32...  21.5 us
    pallas_call x1, Pallas kernels, second_layer(): pl.pallas_call(functools.partial(second_kernel, scale), out_shape=(jax.Sh...  13.6 us
    pallas_call x1, Pallas kernels, first_aggregate(): pl.pallas_call(first_kernel, out_shape=jax.ShapeDtypeStruct((NB, 64, BLK)...  6.73 us

profile of v4, /device:TPU:0, one launch (start us, length us, event | category | flops | bytes accessed | tf_op | source)
XLA Modules:
  0.0 120.4 jit_solution(16043908676775942388)
XLA Ops:
  0.6 0.0 copy-start.1
  0.6 1.2 %copy-done.1 = bf16[8192,64]{0,1:T(8,128)(2,1)S(1)} copy-done((bf16[8192,64]{0,1:T(8,128)(2,1)S(1)}, bf16[8192,64]{0,1:T(8,128)(2,1)}, u32[]{:S(2)}) %copy-start.1) | copy-done | bytes 1048600
  1.9 0.0 copy-start.5
  1.9 0.7 copy-done.5
  2.5 0.0 copy-start
  2.5 0.0 copy-start.7
  2.5 0.0 copy-start.8
  2.5 36.3 %shard_map.111.table = bf16[192,64,128]{2,1,0:T(8,128)(2,1)S(1)} custom-call(s32[2,64]{1,0:T(2,128)S(1)} %bitcast.13, bf16[64,8192]{1,0:T(8,128)(2,1)S(1)} %bitcast.10), custom_call_target="tpu_custom_call" | custom-call | flops 10000000000 | bytes 100000000 | tf_op jit(solution)/shard_map/pallas_call | solution.py:123
  38.8 0.0 copy-done
  38.8 0.0 copy-done.7
  38.8 0.0 copy-done.8
  38.8 0.0 copy-start.2
  38.9 0.0 copy-start.4
  38.9 0.0 copy-start.6
  38.9 6.7 %shard_map.112.mixed = bf16[64,64,128]{2,1,0:T(8,128)(2,1)S(1)} custom-call(s32[256]{0:T(256)S(1)} %copy-done.7, s32[256]{0:T(256)S(1)} %copy-done.8, bf16[256,128,128]{2,1,0:T(8,128)(2,1)S(1)} %copy-done, bf16[192,64,128]{2,1,0:T(8,128)(2,1)S(1)} %shard_map.111.table), custom_call_target="tpu_custom_call" | custom-call | flops 10000000000 | bytes 100000000 | tf_op jit(solution)/shard_map/pallas_call | solution.py:165
  45.6 0.0 copy-done.2
  45.6 0.0 copy-done.4
  45.6 0.0 copy-done.6
  45.7 0.0 copy-start.3
  45.7 36.1 %shard_map.113 = (bf16[192,128,128]{2,1,0:T(8,128)(2,1)S(1)}, bf16[192,128,256]{2,1,0:T(8,128)(2,1)S(1)}, bf16[48,256]{1,0:T(8,128)(2,1)S(1)}) custom-call(s32[2,64]{1,0:T(2,128)S(1)} %bitcast.14, bf16[64,64,128]{2,1,0:T(8,128)(2,1)S(1)} %shard_map.112.mixed, bf16[128,128]{1,0:T(8,128)(2,1)S(1)} %copy-done.2, bf16[47,128]{1,0:T(8,128)(2,1)S(1)} %bitcast.12), custom_call_target="tpu_custom_call" | custom-call | flops 10000000000 | bytes 100000000 | tf_op jit(solution)/shard_map/pallas_call | solution.py:262
  81.8 0.0 copy-done.3
  81.8 13.6 %shard_map.114 = (f32[192,256]{1,0:T(8,128)S(1)}, bf16[64,128,128]{2,1,0:T(8,128)(2,1)}) custom-call(s32[256]{0:T(256)S(1)} %copy-done.7, s32[256]{0:T(256)S(1)} %copy-done.8, s32[8,1,1024]{2,1,0:T(1,128)S(1)} %bitcast.11, bf16[256,128,128]{2,1,0:T(8,128)(2,1)S(1)} %copy-done, bf16[192,128,128]{2,1,0:T(8,128)(2,1)S(1)} %get-tuple-element.9.table, ...), custom_call_target="tpu_custom_call" | custom-call | flops 10000000000 | bytes 100000000 | tf_op jit(solution)/shard_map/pallas_call | solution.py:371
  95.4 21.5 %shard_map.115 = f32[192,128]{1,0:T(8,128)S(1)} custom-call(f32[192,256]{1,0:T(8,128)S(1)} %get-tuple-element.13.pay), custom_call_target="tpu_custom_call" | custom-call | flops 10000000000 | bytes 100000000 | tf_op jit(solution)/shard_map/pallas_call | solution.py:464
  116.8 0.5 slice.11
  118.0 0.6 slice_bitcast_fusion
  118.6 0.6 slice.9
Async XLA Ops:
  0.6 1.2 %copy-start.1 = (bf16[8192,64]{0,1:T(8,128)(2,1)S(1)}, bf16[8192,64]{0,1:T(8,128)(2,1)}, u32[]{:S(2)}) copy-start(bf16[8192,64]{0,1:T(8,128)(2,1)} %param.8) | copy-start | bytes 3145732
  1.9 0.7 copy-start.5
  2.5 36.3 %copy-start = (bf16[256,128,128]{2,1,0:T(8,128)(2,1)S(1)}, bf16[256,128,128]{2,1,0:T(8,128)(2,1)}, u32[]{:S(2)}) copy-start(bf16[256,128,128]{2,1,0:T(8,128)(2,1)} %tiles.3) | copy-start | bytes 25165828
  2.5 36.3 %copy-start.7 = (s32[256]{0:T(256)S(1)}, s32[256]{0:T(256)}, u32[]{:S(2)}) copy-start(s32[256]{0:T(256)} %src_in.3) | copy-start | bytes 3076
  2.5 36.3 %copy-start.8 = (s32[256]{0:T(256)S(1)}, s32[256]{0:T(256)}, u32[]{:S(2)}) copy-start(s32[256]{0:T(256)} %dst_in.3) | copy-start | bytes 3076
  38.8 6.8 %copy-start.2 = (bf16[128,128]{1,0:T(8,128)(2,1)S(1)}, bf16[128,128]{1,0:T(8,128)(2,1)}, u32[]{:S(2)}) copy-start(bf16[128,128]{1,0:T(8,128)(2,1)} %w1.1) | copy-start | bytes 98308
  38.9 6.8 %copy-start.4 = (bf16[128,47]{0,1:T(8,128)(2,1)S(1)}, bf16[128,47]{0,1:T(8,128)(2,1)}, u32[]{:S(2)}) copy-start(bf16[128,47]{0,1:T(8,128)(2,1)} %param.10) | copy-start | bytes 36100
  38.9 6.8 %copy-start.6 = (s32[1,64,2]{1,2,0:T(2,128)S(1)}, s32[1,64,2]{1,2,0:T(2,128)}, u32[]{:S(2)}) copy-start(s32[1,64,2]{1,2,0:T(2,128)} %param.12) | copy-start | bytes 1540
  45.7 36.1 %copy-start.3 = (s32[8192]{0:T(1024)S(1)}, s32[8192]{0:T(1024)}, u32[]{:S(2)}) copy-start(s32[8192]{0:T(1024)} %param.11) | copy-start | bytes 98308

commit v5 on v4

--- a/solution.py
+++ b/solution.py
@@ -248,13 +248,16 @@
             activate(e)
             activate(e + 1)
 
-    take(0)
-
-    @pl.loop(1, (DOM - 1) // BATCH)
+    @pl.loop(0, 2)
     def _(g):
         take(g)
-        finish(g - 1)
-
+
+    @pl.loop(2, (DOM - 1) // BATCH)
+    def _(g):
+        take(g)
+        finish(g - 2)
+
+    finish((DOM - 1) // BATCH - 2)
     finish((DOM - 1) // BATCH - 1)
 
 

time: 121 us -> 117 us (0.967)
  Pallas kernels: 114 us -> 111 us
    pallas_call x1, Pallas kernels: 21.5 us -> 18.5 us  [sum_all(): pl.pallas_call(sum_kernel, out_shape=jax.ShapeDtypeStruct((PAY, BLK), F32...]
    pallas_call x1, Pallas kernels: 36.1 us -> 34.8 us  [exchange_mixed(): pl.pallas_call(mixed_kernel, out_shape=(jax.ShapeDtypeStruct((ENTRIES, BL...]
where the time goes in v5:
time: 117 us
  Pallas kernels  111 us (95%)
  local copies, waits for them, and re-layouts  3.69 us (3%)
  between operations  2.55 us (2%)
    pallas_call x1, Pallas kernels, exchange_features(): pl.pallas_call(feature_kernel, out_shape=jax.ShapeDtypeStruct((ENTRIES, 6...  36.3 us
    pallas_call x1, Pallas kernels, exchange_mixed(): pl.pallas_call(mixed_kernel, out_shape=(jax.ShapeDtypeStruct((ENTRIES, BL...  34.8 us
    pallas_call x1, Pallas kernels, sum_all(): pl.pallas_call(sum_kernel, out_shape=jax.ShapeDtypeStruct((PAY, BLK), F32...  18.5 us
    pallas_call x1, Pallas kernels, second_layer(): pl.pallas_call(functools.partial(second_kernel, scale), out_shape=(jax.Sh...  14.7 us
    pallas_call x1, Pallas kernels, first_aggregate(): pl.pallas_call(first_kernel, out_shape=jax.ShapeDtypeStruct((NB, 64, BLK)...  6.73 us

profile of v5, /device:TPU:0, one launch (start us, length us, event | category | flops | bytes accessed | tf_op | source)
XLA Modules:
  0.0 117.3 jit_solution(12153026581527151870)
XLA Ops:
  0.6 0.0 copy-start.1
  0.6 1.2 %copy-done.1 = bf16[8192,64]{0,1:T(8,128)(2,1)S(1)} copy-done((bf16[8192,64]{0,1:T(8,128)(2,1)S(1)}, bf16[8192,64]{0,1:T(8,128)(2,1)}, u32[]{:S(2)}) %copy-start.1) | copy-done | bytes 1048600
  1.9 0.0 copy-start.5
  1.9 0.7 copy-done.5
  2.5 0.0 copy-start
  2.5 0.0 copy-start.7
  2.5 0.0 copy-start.8
  2.5 36.3 %shard_map.111.table = bf16[192,64,128]{2,1,0:T(8,128)(2,1)S(1)} custom-call(s32[2,64]{1,0:T(2,128)S(1)} %bitcast.13, bf16[64,8192]{1,0:T(8,128)(2,1)S(1)} %bitcast.10), custom_call_target="tpu_custom_call" | custom-call | flops 10000000000 | bytes 100000000 | tf_op jit(solution)/shard_map/pallas_call | solution.py:123
  38.8 0.0 copy-done
  38.8 0.0 copy-done.7
  38.8 0.0 copy-done.8
  38.8 0.0 copy-start.2
  38.9 0.0 copy-start.4
  38.9 0.0 copy-start.6
  38.9 6.7 %shard_map.112.mixed = bf16[64,64,128]{2,1,0:T(8,128)(2,1)S(1)} custom-call(s32[256]{0:T(256)S(1)} %copy-done.7, s32[256]{0:T(256)S(1)} %copy-done.8, bf16[256,128,128]{2,1,0:T(8,128)(2,1)S(1)} %copy-done, bf16[192,64,128]{2,1,0:T(8,128)(2,1)S(1)} %shard_map.111.table), custom_call_target="tpu_custom_call" | custom-call | flops 10000000000 | bytes 100000000 | tf_op jit(solution)/shard_map/pallas_call | solution.py:165
  45.6 0.0 copy-done.2
  45.6 0.0 copy-done.4
  45.6 0.0 copy-done.6
  45.7 0.0 copy-start.3
  45.7 34.8 %shard_map.113 = (bf16[192,128,128]{2,1,0:T(8,128)(2,1)S(1)}, bf16[192,128,256]{2,1,0:T(8,128)(2,1)S(1)}, bf16[48,256]{1,0:T(8,128)(2,1)S(1)}) custom-call(s32[2,64]{1,0:T(2,128)S(1)} %bitcast.14, bf16[64,64,128]{2,1,0:T(8,128)(2,1)S(1)} %shard_map.112.mixed, bf16[128,128]{1,0:T(8,128)(2,1)S(1)} %copy-done.2, bf16[47,128]{1,0:T(8,128)(2,1)S(1)} %bitcast.12), custom_call_target="tpu_custom_call" | custom-call | flops 10000000000 | bytes 100000000 | tf_op jit(solution)/shard_map/pallas_call | solution.py:265
  80.5 0.0 copy-done.3
  80.5 14.7 %shard_map.114 = (f32[192,256]{1,0:T(8,128)S(1)}, bf16[64,128,128]{2,1,0:T(8,128)(2,1)}) custom-call(s32[256]{0:T(256)S(1)} %copy-done.7, s32[256]{0:T(256)S(1)} %copy-done.8, s32[8,1,1024]{2,1,0:T(1,128)S(1)} %bitcast.11, bf16[256,128,128]{2,1,0:T(8,128)(2,1)S(1)} %copy-done, bf16[192,128,128]{2,1,0:T(8,128)(2,1)S(1)} %get-tuple-element.9.table, ...), custom_call_target="tpu_custom_call" | custom-call | flops 10000000000 | bytes 100000000 | tf_op jit(solution)/shard_map/pallas_call | solution.py:374
  95.2 18.5 %shard_map.115 = f32[192,128]{1,0:T(8,128)S(1)} custom-call(f32[192,256]{1,0:T(8,128)S(1)} %get-tuple-element.13.pay), custom_call_target="tpu_custom_call" | custom-call | flops 10000000000 | bytes 100000000 | tf_op jit(solution)/shard_map/pallas_call | solution.py:467
  113.8 0.5 slice.11
  114.9 0.6 slice_bitcast_fusion
  115.5 0.6 slice.9
Async XLA Ops:
  0.6 1.2 %copy-start.1 = (bf16[8192,64]{0,1:T(8,128)(2,1)S(1)}, bf16[8192,64]{0,1:T(8,128)(2,1)}, u32[]{:S(2)}) copy-start(bf16[8192,64]{0,1:T(8,128)(2,1)} %param.8) | copy-start | bytes 3145732
  1.9 0.7 copy-start.5
  2.5 36.3 %copy-start = (bf16[256,128,128]{2,1,0:T(8,128)(2,1)S(1)}, bf16[256,128,128]{2,1,0:T(8,128)(2,1)}, u32[]{:S(2)}) copy-start(bf16[256,128,128]{2,1,0:T(8,128)(2,1)} %tiles.3) | copy-start | bytes 25165828
  2.5 36.3 %copy-start.7 = (s32[256]{0:T(256)S(1)}, s32[256]{0:T(256)}, u32[]{:S(2)}) copy-start(s32[256]{0:T(256)} %src_in.3) | copy-start | bytes 3076
  2.5 36.3 %copy-start.8 = (s32[256]{0:T(256)S(1)}, s32[256]{0:T(256)}, u32[]{:S(2)}) copy-start(s32[256]{0:T(256)} %dst_in.3) | copy-start | bytes 3076
  38.8 6.8 %copy-start.2 = (bf16[128,128]{1,0:T(8,128)(2,1)S(1)}, bf16[128,128]{1,0:T(8,128)(2,1)}, u32[]{:S(2)}) copy-start(bf16[128,128]{1,0:T(8,128)(2,1)} %w1.1) | copy-start | bytes 98308
  38.9 6.8 %copy-start.4 = (bf16[128,47]{0,1:T(8,128)(2,1)S(1)}, bf16[128,47]{0,1:T(8,128)(2,1)}, u32[]{:S(2)}) copy-start(bf16[128,47]{0,1:T(8,128)(2,1)} %param.10) | copy-start | bytes 36100
  38.9 6.8 %copy-start.6 = (s32[1,64,2]{1,2,0:T(2,128)S(1)}, s32[1,64,2]{1,2,0:T(2,128)}, u32[]{:S(2)}) copy-start(s32[1,64,2]{1,2,0:T(2,128)} %param.12) | copy-start | bytes 1540
  45.7 34.8 %copy-start.3 = (s32[8192]{0:T(1024)S(1)}, s32[8192]{0:T(1024)}, u32[]{:S(2)}) copy-start(s32[8192]{0:T(1024)} %param.11) | copy-start | bytes 98308

commit v6 on v5

--- a/solution.py
+++ b/solution.py
@@ -19,7 +19,7 @@
 CPAD = 48
 UNROLL = 16
 BATCH = 3
-MANY = 32
+MANY = 64
 WIDE = 8
 ROWS = WIDE * BLK
 LIST = NT + UNROLL

time: 117 us -> 117 us (level)
    pallas_call x1, Pallas kernels: 14.7 us -> 13.6 us  [second_layer(): pl.pallas_call(functools.partial(second_kernel, scale), out_shape=(jax.Sh...]
    pallas_call x1, Pallas kernels: 18.5 us -> 19.7 us  [sum_all(): pl.pallas_call(sum_kernel, out_shape=jax.ShapeDtypeStruct((PAY, BLK), F32...]
where the time goes in v6:
time: 117 us
  Pallas kernels  111 us (95%)
  local copies, waits for them, and re-layouts  3.69 us (3%)
  between operations  2.55 us (2%)
    pallas_call x1, Pallas kernels, exchange_features(): pl.pallas_call(feature_kernel, out_shape=jax.ShapeDtypeStruct((ENTRIES, 6...  36.3 us
    pallas_call x1, Pallas kernels, exchange_mixed(): pl.pallas_call(mixed_kernel, out_shape=(jax.ShapeDtypeStruct((ENTRIES, BL...  34.8 us
    pallas_call x1, Pallas kernels, sum_all(): pl.pallas_call(sum_kernel, out_shape=jax.ShapeDtypeStruct((PAY, BLK), F32...  19.7 us
    pallas_call x1, Pallas kernels, second_layer(): pl.pallas_call(functools.partial(second_kernel, scale), out_shape=(jax.Sh...  13.6 us
    pallas_call x1, Pallas kernels, first_aggregate(): pl.pallas_call(first_kernel, out_shape=jax.ShapeDtypeStruct((NB, 64, BLK)...  6.3 us

profile of v6, /device:TPU:0, one launch (start us, length us, event | category | flops | bytes accessed | tf_op | source)
XLA Modules:
  0.0 116.9 jit_solution(2352968888699618621)
XLA Ops:
  0.6 0.0 copy-start.1
  0.6 1.2 %copy-done.1 = bf16[8192,64]{0,1:T(8,128)(2,1)S(1)} copy-done((bf16[8192,64]{0,1:T(8,128)(2,1)S(1)}, bf16[8192,64]{0,1:T(8,128)(2,1)}, u32[]{:S(2)}) %copy-start.1) | copy-done | bytes 1048600
  1.9 0.0 copy-start.5
  1.9 0.7 copy-done.5
  2.5 0.0 copy-start
  2.5 0.0 copy-start.7
  2.5 0.0 copy-start.8
  2.5 36.3 %shard_map.111.table = bf16[192,64,128]{2,1,0:T(8,128)(2,1)S(1)} custom-call(s32[2,64]{1,0:T(2,128)S(1)} %bitcast.13, bf16[64,8192]{1,0:T(8,128)(2,1)S(1)} %bitcast.10), custom_call_target="tpu_custom_call" | custom-call | flops 10000000000 | bytes 100000000 | tf_op jit(solution)/shard_map/pallas_call | solution.py:123
  38.8 0.0 copy-done
  38.8 0.0 copy-done.7
  38.8 0.0 copy-done.8
  38.8 0.0 copy-start.2
  38.9 0.0 copy-start.4
  38.9 0.0 copy-start.6
  38.9 6.3 %shard_map.112.mixed = bf16[64,64,128]{2,1,0:T(8,128)(2,1)S(1)} custom-call(s32[256]{0:T(256)S(1)} %copy-done.7, s32[256]{0:T(256)S(1)} %copy-done.8, bf16[256,128,128]{2,1,0:T(8,128)(2,1)S(1)} %copy-done, bf16[192,64,128]{2,1,0:T(8,128)(2,1)S(1)} %shard_map.111.table), custom_call_target="tpu_custom_call" | custom-call | flops 10000000000 | bytes 100000000 | tf_op jit(solution)/shard_map/pallas_call | solution.py:165
  45.2 0.0 copy-done.2
  45.2 0.0 copy-done.4
  45.2 0.0 copy-done.6
  45.2 0.0 copy-start.3
  45.2 34.8 %shard_map.113 = (bf16[192,128,128]{2,1,0:T(8,128)(2,1)S(1)}, bf16[192,128,256]{2,1,0:T(8,128)(2,1)S(1)}, bf16[48,256]{1,0:T(8,128)(2,1)S(1)}) custom-call(s32[2,64]{1,0:T(2,128)S(1)} %bitcast.14, bf16[64,64,128]{2,1,0:T(8,128)(2,1)S(1)} %shard_map.112.mixed, bf16[128,128]{1,0:T(8,128)(2,1)S(1)} %copy-done.2, bf16[47,128]{1,0:T(8,128)(2,1)S(1)} %bitcast.12), custom_call_target="tpu_custom_call" | custom-call | flops 10000000000 | bytes 100000000 | tf_op jit(solution)/shard_map/pallas_call | solution.py:265
  80.0 0.0 copy-done.3
  80.1 13.6 %shard_map.114 = (f32[192,256]{1,0:T(8,128)S(1)}, bf16[64,128,128]{2,1,0:T(8,128)(2,1)}) custom-call(s32[256]{0:T(256)S(1)} %copy-done.7, s32[256]{0:T(256)S(1)} %copy-done.8, s32[8,1,1024]{2,1,0:T(1,128)S(1)} %bitcast.11, bf16[256,128,128]{2,1,0:T(8,128)(2,1)S(1)} %copy-done, bf16[192,128,128]{2,1,0:T(8,128)(2,1)S(1)} %get-tuple-element.9.table, ...), custom_call_target="tpu_custom_call" | custom-call | flops 10000000000 | bytes 100000000 | tf_op jit(solution)/shard_map/pallas_call | solution.py:374
  93.6 19.7 %shard_map.115 = f32[192,128]{1,0:T(8,128)S(1)} custom-call(f32[192,256]{1,0:T(8,128)S(1)} %get-tuple-element.13.pay), custom_call_target="tpu_custom_call" | custom-call | flops 10000000000 | bytes 100000000 | tf_op jit(solution)/shard_map/pallas_call | solution.py:467
  113.3 0.5 slice.11
  114.5 0.6 slice_bitcast_fusion
  115.1 0.6 slice.9
Async XLA Ops:
  0.6 1.2 %copy-start.1 = (bf16[8192,64]{0,1:T(8,128)(2,1)S(1)}, bf16[8192,64]{0,1:T(8,128)(2,1)}, u32[]{:S(2)}) copy-start(bf16[8192,64]{0,1:T(8,128)(2,1)} %param.8) | copy-start | bytes 3145732
  1.9 0.7 copy-start.5
  2.5 36.3 %copy-start = (bf16[256,128,128]{2,1,0:T(8,128)(2,1)S(1)}, bf16[256,128,128]{2,1,0:T(8,128)(2,1)}, u32[]{:S(2)}) copy-start(bf16[256,128,128]{2,1,0:T(8,128)(2,1)} %tiles.3) | copy-start | bytes 25165828
  2.5 36.3 %copy-start.7 = (s32[256]{0:T(256)S(1)}, s32[256]{0:T(256)}, u32[]{:S(2)}) copy-start(s32[256]{0:T(256)} %src_in.3) | copy-start | bytes 3076
  2.5 36.3 %copy-start.8 = (s32[256]{0:T(256)S(1)}, s32[256]{0:T(256)}, u32[]{:S(2)}) copy-start(s32[256]{0:T(256)} %dst_in.3) | copy-start | bytes 3076
  38.8 6.3 %copy-start.2 = (bf16[128,128]{1,0:T(8,128)(2,1)S(1)}, bf16[128,128]{1,0:T(8,128)(2,1)}, u32[]{:S(2)}) copy-start(bf16[128,128]{1,0:T(8,128)(2,1)} %w1.1) | copy-start | bytes 98308
  38.9 6.3 %copy-start.4 = (bf16[128,47]{0,1:T(8,128)(2,1)S(1)}, bf16[128,47]{0,1:T(8,128)(2,1)}, u32[]{:S(2)}) copy-start(bf16[128,47]{0,1:T(8,128)(2,1)} %param.10) | copy-start | bytes 36100
  38.9 6.3 %copy-start.6 = (s32[1,64,2]{1,2,0:T(2,128)S(1)}, s32[1,64,2]{1,2,0:T(2,128)}, u32[]{:S(2)}) copy-start(s32[1,64,2]{1,2,0:T(2,128)} %param.12) | copy-start | bytes 1540
  45.2 34.8 %copy-start.3 = (s32[8192]{0:T(1024)S(1)}, s32[8192]{0:T(1024)}, u32[]{:S(2)}) copy-start(s32[8192]{0:T(1024)} %param.11) | copy-start | bytes 98308
